TPU v7x, 256 devices: a whole 4x4x8 slice. The times are simulated.
256 devices in a mesh: rows: 32 (over y, x, core), cols: 8 (over z).
Axes of the slice: x: 4, y: 4, z: 8, core: 2. Of those that a mesh axis runs over, the one named last changes fastest.
Arguments:
- a_blocks: bfloat16 [8192, 28672], P(('rows', 'cols')), may hold values from -6 to 6
- prolong: bfloat16 [8192, 4096], P(('rows', 'cols')), may hold values from -0.75 to 0.75
- columns: int32 [8192, 7], P(('rows', 'cols')), may hold values from -1 to 8191, as said below
- aggregate: int32 [8192], P(('rows', 'cols')), may hold values from 0 to 3, as said below
Outputs:
- coarse: float32 [1024, 64, 320], P('rows', 'cols')
Inputs may be any that keep to these rules, and one draw needn't show every extreme that they name: `columns`: entries that are not -1 lie within 8 block rows of their own row, and some lie exactly 8 away on each side; -1 marks padding, placed at random positions of a row. Within each block of 32 rows the ids never fall, every id 0 to 3 is used, and each aggregate has 4 to 12 rows, both reached in every such block; so glob of a valid column differs from the row's by at most 2.
All inputs are finite; a program needn't handle non-finite values.
Results may differ from a plain program's by a relative error of at most 0.0029.
Values may be sent and summed in bfloat16 or wider, within the bound.
No kernel may reach another device: no remote copies, remote signals or barrier semaphores. Data moves between devices by JAX's collectives and lax.ppermute only.
A program may use at most 64 MiB of HBM per device.

v0:
```python
import jax
import jax.numpy as jnp
from jax import lax
from jax.sharding import PartitionSpec as P

BW = 64
NS = 64
KN = 7
RC = 2
SL = 5
LA = 4


def from_behind(shard, axis, by):
    length = lax.axis_size(axis)
    pairs = [(i, i + by) for i in range(length) if 0 <= i + by < length]
    return lax.ppermute(shard, axis, pairs)


def shards(a_blocks, prolong, columns, aggregate):
    count = prolong.shape[0]
    device = lax.axis_index(("rows", "cols"))
    start = device * count
    own_glob = device * LA + aggregate
    below = from_behind((prolong, own_glob), ("rows", "cols"), 1)
    above = from_behind((prolong, own_glob), ("rows", "cols"), -1)
    ext_p = jnp.concatenate([below[0], prolong, above[0]], axis=0)
    ext_g = jnp.concatenate([below[1], own_glob, above[1]], axis=0)
    valid = columns >= 0
    where_ext = jnp.where(valid, columns - start + count, count)
    gathered = ext_p[where_ext].reshape(count, KN, BW, NS)
    a_rows = a_blocks.reshape(count, KN, BW, BW)
    prod = jnp.einsum("tkuw,tkwv->tkuv", a_rows, gathered, preferred_element_type=jnp.float32)
    slot = ext_g[where_ext] - own_glob[:, None] + RC
    slot_ids = jnp.arange(SL, dtype=jnp.int32)
    summed_k = jnp.zeros((count, SL, BW, NS), jnp.float32)
    for entry in range(KN):
        match = (slot[:, entry][:, None] == slot_ids[None, :]) & valid[:, entry][:, None]
        summed_k = summed_k + jnp.where(match[:, :, None, None], prod[:, entry][:, None, :, :], 0.0)
    grouped = summed_k.astype(jnp.bfloat16)
    own_p = prolong.reshape(count, BW, NS)
    local = jnp.einsum("twu,tswv->tsuv", own_p, grouped, preferred_element_type=jnp.float32)
    per_aggr = jax.ops.segment_sum(local, aggregate, num_segments=LA, indices_are_sorted=True)
    summed = jnp.transpose(per_aggr, (0, 3, 1, 2)).reshape(LA, NS, SL * NS)
    return lax.all_to_all(summed, "cols", split_axis=1, concat_axis=0, tiled=True)


def solution(mesh):
    in_specs = (
        P(("rows", "cols"), None),
        P(("rows", "cols"), None),
        P(("rows", "cols"), None),
        P(("rows", "cols")),
    )
    out_specs = P("rows", "cols", None)
    return jax.shard_map(shards, mesh=mesh, in_specs=in_specs, out_specs=out_specs, check_vma=False)
```

profile of v0, /device:TPU:6, one launch (start us, length us, event | category | flops | bytes accessed | tf_op | source)
XLA Modules:
  0.0 82.4 jit_solution(12151539931671264085)
XLA Ops:
  0.0 0.7 broadcast_add_fusion
  0.7 3.8 %collective-permute-start = (s32[32]{0:T(128)S(1)}, s32[32]{0:T(128)S(1)}, u32[]{:S(2)}, u32[]{:S(2)}) collective-permute-start(s32[32]{0:T(128)S(1)} %broadcast_add_fusion), channel_id=1, source_target_pairs={{0,1},{1,2},{2,3},{3,4},{4,5},{5,6},{6,7},{7,8},{8,9},{9,10},{10,1... | collective-permute-start | bytes 392 | tf_op jit(solution)/shard_map/ppermute | solution.py:17
  4.5 5.6 %collective-permute-start.1 = (s32[32]{0:T(128)S(1)}, s32[32]{0:T(128)S(1)}, u32[]{:S(2)}, u32[]{:S(2)}) collective-permute-start(s32[32]{0:T(128)S(1)} %broadcast_add_fusion), channel_id=1, source_target_pairs={{1,0},{2,1},{3,2},{4,3},{5,4},{6,5},{7,6},{8,7},{9,8},{10,9},{11,1... | collective-permute-start | bytes 392 | tf_op jit(solution)/shard_map/ppermute | solution.py:17
  10.1 1.9 %collective-permute-start.2 = (bf16[32,4096]{1,0:T(8,128)(2,1)}, bf16[32,4096]{1,0:T(8,128)(2,1)S(1)}, u32[]{:S(2)}, u32[]{:S(2)}) collective-permute-start(bf16[32,4096]{1,0:T(8,128)(2,1)} %param.5), channel_id=1, source_target_pairs={{0,1},{1,2},{2,3},{3,4},{4,5},{5,6},{6,7},{7,8},{8,9},{9,10},{10,1... | collective-permute-start | bytes 786440 | tf_op jit(solution)/shard_map/ppermute | solution.py:17
  12.0 5.8 %collective-permute-start.3 = (bf16[32,4096]{1,0:T(8,128)(2,1)}, bf16[32,4096]{1,0:T(8,128)(2,1)S(1)}, u32[]{:S(2)}, u32[]{:S(2)}) collective-permute-start(bf16[32,4096]{1,0:T(8,128)(2,1)} %param.5), channel_id=1, source_target_pairs={{1,0},{2,1},{3,2},{4,3},{5,4},{6,5},{7,6},{8,7},{9,8},{10,9},{11,1... | collective-permute-start | bytes 786440 | tf_op jit(solution)/shard_map/ppermute | solution.py:17
  17.7 1.5 %reshape.320 = bf16[32,64,64,1]{2,1,0,3:T(8,128)(2,1)S(1)} reshape(bf16[32,4096]{1,0:T(8,128)(2,1)} %param.5) | data formatting | bytes 524288 | tf_op jit(solution)/shard_map/reshape | solution.py:41
  19.2 0.7 broadcast_compare_fusion
  19.9 0.7 compare_select_fusion
  20.6 0.1 copy.17
  20.7 0.1 reshape.292
  20.8 6.0 %reshape.287 = bf16[32,7,64,64]{3,2,1,0:T(8,128)(2,1)} reshape(bf16[32,28672]{1,0:T(8,128)(2,1)} %param.4) | data formatting | bytes 3670016 | tf_op jit(solution)/shard_map/reshape | solution.py:32
  26.9 0.0 collective-permute-done
  26.9 0.0 collective-permute-done.1
  26.9 0.1 pad_add_fusion
  27.0 0.0 copy-start
  27.0 1.9 %gather_fusion = s32[224]{0:T(256)S(1)} fusion(s32[96]{0:T(128)S(1)} %pad_add_fusion, s32[1024]{0:T(1024)S(1)} %pad_clamp_fusion), kind=kCustom, calls=%fused_computation | custom fusion | bytes 2688 | tf_op jit(solution)/shard_map/gather | solution.py:34
  28.8 0.1 reshape.291
  28.9 0.1 subtract_add_fusion
  29.0 0.3 slice_reduce_fusion.6
  29.3 0.1 fusion.18
  29.4 0.1 fusion.20
  29.5 0.1 fusion.24
  29.6 0.1 fusion.22
  29.7 0.0 collective-permute-done.2
  29.7 0.0 collective-permute-done.3
  29.7 0.0 copy-done
  29.7 0.1 pad_maximum_fusion
  29.7 1.7 %gather_fusion.1 = bf16[224,4096]{1,0:T(8,128)(2,1)S(1)} fusion(bf16[96,4096]{1,0:T(8,128)(2,1)S(1)} %pad_maximum_fusion, s32[1024]{0:T(1024)S(1)} %pad_clamp_fusion), kind=kCustom, calls=%fused_computation.1 | custom fusion | bytes 3670912 | tf_op jit(solution)/shard_map/gather | solution.py:31
  31.4 5.0 %reshape.286 = bf16[32,7,64,64]{3,2,1,0:T(8,128)(2,1)} reshape(bf16[224,4096]{1,0:T(8,128)(2,1)S(1)} %gather_fusion.1) | data formatting | bytes 3670016 | tf_op jit(solution)/shard_map/reshape | solution.py:31
  36.4 5.2 %convolution_bitcast_fusion = f32[32,7,64,64]{2,3,1,0:T(8,128)S(1)} fusion(bf16[32,7,64,64]{3,2,1,0:T(8,128)(2,1)} %reshape.286, bf16[32,7,64,64]{3,2,1,0:T(8,128)(2,1)} %reshape.287), kind=kOutput, calls=%fused_computation.4 | convolution fusion | flops 117440512 | bytes 7340032 | tf_op jit(solution)/shard_map/tkuw,tkwv->tkuv/dot_general | solution.py:33
  41.6 1.2 %slice_bitcast_fusion.6 = (f32[32,64,64]{1,2,0:T(8,128)S(1)}, f32[32,64,64]{1,2,0:T(8,128)S(1)}, f32[32,64,64]{1,2,0:T(8,128)S(1)}, f32[32,64,64]{1,2,0:T(8,128)...) fusion(f32[32,7,64,64]{2,3,1,0:T(8,128)S(1)} %convolution_bitcast_fusion), kind=kLoop, calls=%fused_computation.28 | loop fusion | bytes 7340032 | tf_op jit(solution)/shard_map/jit(_where)/broadcast_in_dim | solution.py:39
  42.8 6.3 %fusion.16 = f32[32,5,64,64]{2,3,1,0:T(8,128)} fusion(f32[32,64,64]{1,2,0:T(8,128)S(1)} %get-tuple-element.13, f32[32,64,64]{1,2,0:T(8,128)S(1)} %get-tuple-element.14, f32[32,64,64]{1,2,0:T(8,128)S(1)} %get-tuple-element.15, f32[32,64,64]{1,2,0:T(8,128)S(1)} %get-tuple-element.16, f32[32,64,64]{1,2,0:T(8,128)S(1)} %get-tuple-element.17, ...), kind=kOutput, calls=%fused_computation.21 | convolution fusion | flops 93061120 | bytes 6554720 | tf_op jit(solution)/shard_map/twu,tswv->tsuv/dot_general | solution.py:42
  49.2 0.0 copy-start.1
  49.2 6.0 %copy.19 = f32[32,5,64,64]{3,2,1,0:T(8,128)} copy(f32[32,5,64,64]{2,3,1,0:T(8,128)} %fusion.16) | data formatting | bytes 5242880 | tf_op jit(solution)/shard_map/twu,tswv->tsuv/transpose | solution.py:42
  55.1 0.1 broadcast_in_dim.127
  55.2 0.0 copy-done.1
  55.2 7.2 %scatter_fusion = f32[4,5,64,64]{3,2,1,0:T(8,128)S(1)} fusion(f32[4,5,64,64]{3,2,1,0:T(8,128)S(1)} %broadcast_in_dim.127, s32[32]{0:T(128)S(1)} %copy-done.1, f32[32,5,64,64]{3,2,1,0:T(8,128)} %copy.19), kind=kCustom, calls=%fused_computation.2 | custom fusion | flops 655360 | bytes 7864448 | tf_op jit(solution)/shard_map/scatter-add | solution.py:43
  62.5 0.3 copy.20
  62.7 18.9 %all_to_all.18 = f32[4,64,320]{2,0,1:T(4,128)S(1)} all-to-all(f32[4,64,320]{2,0,1:T(4,128)S(1)} %copy.20), channel_id=1, replica_groups=mesh['rows'=32,'cols'=8] {'cols'}, dimensions={1} | all-to-all | bytes 655360 | tf_op jit(solution)/shard_map/all_to_all | solution.py:45
  81.6 0.8 copy.22
  (3 shorter events, 0.0 us)
Async XLA Ops:
  0.7 26.2 %collective-permute-start = (s32[32]{0:T(128)S(1)}, s32[32]{0:T(128)S(1)}, u32[]{:S(2)}, u32[]{:S(2)}) collective-permute-start(s32[32]{0:T(128)S(1)} %broadcast_add_fusion), channel_id=1, source_target_pairs={{0,1},{1,2},{2,3},{3,4},{4,5},{5,6},{6,7},{7,8},{8,9},{9,10},{10,1... | collective-permute-start | bytes 392 | tf_op jit(solution)/shard_map/ppermute | solution.py:17
  4.5 22.4 %collective-permute-start.1 = (s32[32]{0:T(128)S(1)}, s32[32]{0:T(128)S(1)}, u32[]{:S(2)}, u32[]{:S(2)}) collective-permute-start(s32[32]{0:T(128)S(1)} %broadcast_add_fusion), channel_id=1, source_target_pairs={{1,0},{2,1},{3,2},{4,3},{5,4},{6,5},{7,6},{8,7},{9,8},{10,9},{11,1... | collective-permute-start | bytes 392 | tf_op jit(solution)/shard_map/ppermute | solution.py:17
  10.1 19.6 %collective-permute-start.2 = (bf16[32,4096]{1,0:T(8,128)(2,1)}, bf16[32,4096]{1,0:T(8,128)(2,1)S(1)}, u32[]{:S(2)}, u32[]{:S(2)}) collective-permute-start(bf16[32,4096]{1,0:T(8,128)(2,1)} %param.5), channel_id=1, source_target_pairs={{0,1},{1,2},{2,3},{3,4},{4,5},{5,6},{6,7},{7,8},{8,9},{9,10},{10,1... | collective-permute-start | bytes 786440 | tf_op jit(solution)/shard_map/ppermute | solution.py:17
  12.0 17.7 %collective-permute-start.3 = (bf16[32,4096]{1,0:T(8,128)(2,1)}, bf16[32,4096]{1,0:T(8,128)(2,1)S(1)}, u32[]{:S(2)}, u32[]{:S(2)}) collective-permute-start(bf16[32,4096]{1,0:T(8,128)(2,1)} %param.5), channel_id=1, source_target_pairs={{1,0},{2,1},{3,2},{4,3},{5,4},{6,5},{7,6},{8,7},{9,8},{10,9},{11,1... | collective-permute-start | bytes 786440 | tf_op jit(solution)/shard_map/ppermute | solution.py:17
  27.0 2.7 %copy-start = (bf16[32,4096]{1,0:T(8,128)(2,1)S(1)}, bf16[32,4096]{1,0:T(8,128)(2,1)}, u32[]{:S(2)}) copy-start(bf16[32,4096]{1,0:T(8,128)(2,1)} %param.5) | copy-start | bytes 786436
  49.2 6.0 %copy-start.1 = (s32[32]{0:T(128)S(1)}, s32[32]{0:T(128)}, u32[]{:S(2)}) copy-start(s32[32]{0:T(128)} %param.7) | copy-start | bytes 388
where the time goes:
time: 83 us; the launch traced here: 82.4 us
  local copies, waits for them, and re-layouts  24.9 us (30%)
  blocking collectives  18.9 us (23%)
  starting transfers between devices  17.1 us (21%)
  matrix products  11.6 us (14%)
  other arithmetic  9.83 us (12%)
    all_to_all x1, blocking collectives, shards(): lax.all_to_all(summed, 'cols', split_axis=1, concat_axis=0, tiled=True)  18.9 us
    ppermute x4, starting transfers between devices, from_behind(): return lax.ppermute(shard, axis, pairs)  17.1 us
    scatter-add x1, other arithmetic, shards(): jax.ops.segment_sum(local, aggregate, num_segments=LA, indices_are_sorted...  7.24 us
    dot_general x1, matrix products, shards(): jnp.einsum('twu,tswv->tsuv', own_p, grouped, preferred_element_type=jnp.f...  6.35 us
    reshape x1, local copies, waits for them, and re-layouts, shards(): a_rows = a_blocks.reshape(count, KN, BW, BW)  6.04 us
    transpose x1, local copies, waits for them, and re-layouts, shards(): jnp.einsum('twu,tswv->tsuv', own_p, grouped, preferred_element_type=jnp.f...  5.97 us
    dot_general x1, matrix products, shards(): jnp.einsum('tkuw,tkwv->tkuv', a_rows, gathered, preferred_element_type=jn...  5.22 us
    reshape x1, local copies, waits for them, and re-layouts, shards(): gathered = ext_p[where_ext].reshape(count, KN, BW, NS)  4.96 us
  transfers between devices with their start and end apart: 4, of which 0 were waited for; matrix products, arithmetic and copies ran while one was open for 14% of the time, Pallas kernels for 0%

commit v1 on v0

v1 whole, which is shorter than its diff:
```python
import jax
import jax.numpy as jnp
from jax import lax
from jax.experimental import pallas as pl
from jax.experimental.pallas import tpu as pltpu
from jax.sharding import PartitionSpec as P

BW = 64
NS = 64
KN = 7
HW = 8
RC = 2
SL = 5
LA = 4
NB = 32
G = 32
EXT = NB + 2 * HW
BLK = BW * BW
COLS = 8


def shifted(shard, by):
    axis = ("rows", "cols")
    length = lax.axis_size(axis)
    return lax.ppermute(shard, axis, [(i, (i + by) % length) for i in range(length)])


def halo_of(prolong, aggregate, rows):
    ids = jnp.broadcast_to(aggregate[rows].astype(jnp.bfloat16)[:, None], (HW, 128))
    return jnp.concatenate([prolong[rows], ids], axis=1)


def local_kernel(start_ref, cols_ref, agg_ref, a_hbm, p_ref, lo_ref, hi_ref, out_ref,
                 a_vmem, a_nat, p_nat, w_wide, w_blk, p_sel, acc, glob, y_buf, sems):
    copies = [
        pltpu.make_async_copy(a_hbm.at[:, pl.ds(k * BLK, BLK)], a_vmem.at[:, pl.ds(k * BLK, BLK)], sems.at[k])
        for k in range(KN)
    ]
    for c in copies:
        c.start()
    start = start_ref[0]

    below = jnp.max(jnp.sum((lo_ref[:, pl.ds(BLK, 128)].astype(jnp.float32) > 2.5).astype(jnp.float32), axis=0)).astype(jnp.int32)
    above = jnp.max(jnp.sum((hi_ref[:, pl.ds(BLK, 128)].astype(jnp.float32) < 0.5).astype(jnp.float32), axis=0)).astype(jnp.int32)
    for t in range(HW):
        glob[t] = jnp.where(HW - t <= below, -1, -2)
        glob[HW + NB + t] = jnp.where(t < above, LA, LA + 1)
    for t in range(NB):
        glob[HW + t] = agg_ref[t]

    for h in range(G):
        lanes = pl.ds(h * 128, 128)
        p_nat[pl.ds(h * EXT, HW), :] = lo_ref[:, lanes].astype(jnp.float32)
        p_nat[pl.ds(h * EXT + HW, NB), :] = p_ref[:, lanes].astype(jnp.float32)
        p_nat[pl.ds(h * EXT + HW + NB, HW), :] = hi_ref[:, lanes].astype(jnp.float32)
    low = lax.broadcasted_iota(jnp.int32, (G, 128), 1) < NS
    p_sel[...] = jnp.zeros_like(p_sel)
    for j in range(EXT):
        nat = p_nat[pl.ds(j, G, stride=EXT), :]
        even = jnp.where(low, nat, 0.0)
        odd = jnp.where(low, 0.0, nat)
        w_wide[j, pl.ds(0, G, stride=2), :] = even
        w_wide[j, pl.ds(1, G, stride=2), :] = pltpu.roll(odd, NS, 1)
        w_wide[j, pl.ds(BW, G, stride=2), :] = pltpu.roll(even, NS, 1)
        w_wide[j, pl.ds(BW + 1, G, stride=2), :] = odd
        w_blk[j] = w_wide[j].astype(jnp.bfloat16)
        if HW <= j < HW + NB:
            i = j - HW
            lane = pl.multiple_of(agg_ref[i] * 128, 128)
            p_sel[pl.ds(i * G, G), pl.ds(lane, 128)] = nat.astype(jnp.bfloat16)
    w_blk[EXT] = jnp.zeros((128, 128), jnp.bfloat16)
    acc[...] = jnp.zeros_like(acc)

    for k in range(KN):
        copies[k].wait()
        for g in range(G):
            a_nat[k, pl.ds(g * NB, NB), :] = a_vmem[:, pl.ds(k * BLK + g * 128, 128)].astype(jnp.float32)
        for i in range(NB):
            block = a_nat[k, pl.ds(i, G, stride=NB), :].astype(jnp.bfloat16)
            col = cols_ref[k, i]
            valid = col >= 0
            j = jnp.where(valid, col - start + HW, EXT)
            slot = jnp.where(valid, glob[jnp.where(valid, j, 0)] - agg_ref[i] + RC, RC)
            prod = jnp.dot(block, w_blk[j], preferred_element_type=jnp.float32)
            lane = pl.multiple_of(slot * 128, 128)
            acc[pl.ds(i * G, G), pl.ds(lane, 128)] += prod

    full = lax.dot_general(acc[...].astype(jnp.bfloat16), p_sel[...], (((0,), (0,)), ((), ())),
                           preferred_element_type=jnp.float32)
    low = lax.broadcasted_iota(jnp.int32, (NS, 128), 1) < NS
    for c in range(LA):
        cc = full[:, c * 128:(c + 1) * 128]
        part = lambda s, par: cc[s * 128 + par * NS:s * 128 + (par + 1) * NS]
        for pair in range(3):
            s0, s1 = 2 * pair, min(2 * pair + 1, SL - 1)
            stay = jnp.where(low, part(s0, 0), part(s1, 1))
            move = jnp.where(low, part(s1, 0), part(s0, 1))
            both = stay + pltpu.roll(move, NS, 1)
            y_buf[:, pl.ds(c * 8, 8), pl.ds(pair * 128, 128)] = both.reshape(8, 8, 128)
    out_ref[...] = y_buf[:, :, :SL * NS].astype(jnp.bfloat16)


def local_part(start, columns_t, aggregate, a_blocks, prolong, lo, hi):
    vmem = pl.BlockSpec(memory_space=pltpu.VMEM)
    smem = pl.BlockSpec(memory_space=pltpu.SMEM)
    return pl.pallas_call(
        local_kernel,
        out_shape=jax.ShapeDtypeStruct((COLS, LA * NS // COLS, SL * NS), jnp.bfloat16),
        in_specs=[smem, smem, smem, pl.BlockSpec(memory_space=pl.ANY), vmem, vmem, vmem],
        out_specs=vmem,
        scratch_shapes=[
            pltpu.VMEM((NB, KN * BLK), jnp.bfloat16),
            pltpu.VMEM((KN, G * NB, 128), jnp.float32),
            pltpu.VMEM((G * EXT, 128), jnp.float32),
            pltpu.VMEM((EXT, 128, 128), jnp.float32),
            pltpu.VMEM((EXT + 1, 128, 128), jnp.bfloat16),
            pltpu.VMEM((NB * G, LA * 128), jnp.bfloat16),
            pltpu.VMEM((NB * G, SL * 128), jnp.float32),
            pltpu.SMEM((EXT,), jnp.int32),
            pltpu.VMEM((COLS, LA * NS // COLS, 3 * 128), jnp.float32),
            pltpu.SemaphoreType.DMA((KN,)),
        ],
        compiler_params=pltpu.CompilerParams(vmem_limit_bytes=40 * 1024 * 1024),
    )(start, columns_t, aggregate, a_blocks, prolong, lo, hi)


def shards(a_blocks, prolong, columns, aggregate):
    count = prolong.shape[0]
    device = lax.axis_index(("rows", "cols"))
    start = (device * count).astype(jnp.int32).reshape(1)
    lo = shifted(halo_of(prolong, aggregate, slice(count - HW, count)), 1)
    hi = shifted(halo_of(prolong, aggregate, slice(0, HW)), -1)
    mine = local_part(start, columns.T, aggregate, a_blocks, prolong, lo, hi)
    landed = lax.all_to_all(mine, "cols", split_axis=0, concat_axis=0, tiled=True)
    return landed.astype(jnp.float32).reshape(COLS * LA, NS // COLS, SL * NS)


def solution(mesh):
    in_specs = (
        P(("rows", "cols"), None),
        P(("rows", "cols"), None),
        P(("rows", "cols"), None),
        P(("rows", "cols")),
    )
    out_specs = P("rows", "cols", None)
    return jax.shard_map(shards, mesh=mesh, in_specs=in_specs, out_specs=out_specs, check_vma=False)
```

time: 83 us -> 39.6 us (0.48)
  the two profiles are of different devices: /device:TPU:6 before, /device:TPU:31 now
where the time goes in v1:
time: 39.6 us; the launch traced here: 39.4 us
  blocking collectives  18.3 us (46%)
  Pallas kernels  6.65 us (17%)
  starting transfers between devices  6.23 us (16%)
  local copies, waits for them, and re-layouts  4.89 us (12%)
  waiting for transfers between devices  1.84 us (5%)
  other arithmetic  1.45 us (4%)
    all_to_all x1, blocking collectives, shards(): lax.all_to_all(mine, 'cols', split_axis=0, concat_axis=0, tiled=True)  18.3 us
    pallas_call x1, Pallas kernels, local_part(): pl.pallas_call(local_kernel, out_shape=jax.ShapeDtypeStruct((COLS, LA * N...  6.65 us
    ppermute x2, starting transfers between devices, shifted(): lax.ppermute(shard, axis, [(i, (i + by) % length) for i in range(length)])  6.23 us
    unnamed x8, local copies, waits for them, and re-layouts  3.79 us
    ppermute x2, waiting for transfers between devices, shifted(): lax.ppermute(shard, axis, [(i, (i + by) % length) for i in range(length)])  1.84 us
    slice x1, local copies, waits for them, and re-layouts, halo_of(): return jnp.concatenate([prolong[rows], ids], axis=1)  0.88 us
  transfers between devices with their start and end apart: 2, of which 1 were waited for; matrix products, arithmetic and copies ran while one was open for 0% of the time, Pallas kernels for 0%

profile of v1, /device:TPU:31, one launch (start us, length us, event | category | flops | bytes accessed | tf_op | source)
XLA Modules:
  0.0 39.4 jit_solution(7641930849139170515)
XLA Ops:
  0.0 0.7 %convert.5 = bf16[32]{0:T(256)(128)(2,1)S(1)} convert(s32[32]{0:T(128)} %agg_ref.1) | non-fusion elementwise | flops 32 | bytes 192 | tf_op jit(solution)/shard_map/convert.2
  0.7 0.1 fusion.1
  0.7 0.9 %fusion = (bf16[8,4096]{1,0:T(8,128)(2,1)S(1)}, bf16[8,4096]{1,0:T(8,128)(2,1)S(1)}) fusion(bf16[32,4096]{1,0:T(8,128)(2,1)} %p_ref.1), kind=kLoop, calls=%fused_computation.2 | loop fusion | bytes 262144 | tf_op jit(solution)/shard_map/slice | solution.py:30
  1.6 0.1 broadcast_in_dim.4
  1.7 1.7 %collective-permute-start = (bf16[8,4224]{1,0:T(8,128)(2,1)S(1)}, bf16[8,4224]{1,0:T(8,128)(2,1)S(1)}, u32[]{:S(2)}, u32[]{:S(2)}) collective-permute-start(bf16[8,4224]{1,0:T(8,128)(2,1)S(1)} %pad_maximum_fusion), channel_id=1, source_target_pairs={{0,1},{1,2},{2,3},{3,4},{4,5},{5,6},{6,7},{7,8},{8,9},{9,10},{10,1... | collective-permute-start | bytes 202760 | tf_op jit(solution)/shard_map/ppermute | solution.py:25
  3.4 0.1 broadcast_in_dim.5
  3.5 4.6 %collective-permute-start.1 = (bf16[8,4224]{1,0:T(8,128)(2,1)S(1)}, bf16[8,4224]{1,0:T(8,128)(2,1)S(1)}, u32[]{:S(2)}, u32[]{:S(2)}) collective-permute-start(bf16[8,4224]{1,0:T(8,128)(2,1)S(1)} %pad_maximum_fusion.1), channel_id=1, source_target_pairs={{0,255},{1,0},{2,1},{3,2},{4,3},{5,4},{6,5},{7,6},{8,7},{9,8},{10,... | collective-permute-start | bytes 202760 | tf_op jit(solution)/shard_map/ppermute | solution.py:25
  8.0 1.8 %collective-permute-done.lo_ref = bf16[8,4224]{1,0:T(8,128)(2,1)S(1)} collective-permute-done((bf16[8,4224]{1,0:T(8,128)(2,1)S(1)}, bf16[8,4224]{1,0:T(8,128)(2,1)S(1)}, u32[]{:S(2)}, u32[]{:S(2)}) %collective-permute-start) | collective-permute-done | bytes 67616 | tf_op jit(solution)/shard_map/ppermute | solution.py:25
  9.9 0.0 collective-permute-done.1.hi_ref
  9.9 0.0 copy-start
  9.9 1.5 %copy-done = bf16[32,28672]{1,0:T(8,128)(2,1)S(1)} copy-done((bf16[32,28672]{1,0:T(8,128)(2,1)S(1)}, bf16[32,28672]{1,0:T(8,128)(2,1)}, u32[]{:S(2)}) %copy-start) | copy-done | bytes 1835032
  11.4 0.0 copy-start.1
  11.4 0.9 %copy-done.1 = bf16[32,4096]{1,0:T(8,128)(2,1)S(1)} copy-done((bf16[32,4096]{1,0:T(8,128)(2,1)S(1)}, bf16[32,4096]{1,0:T(8,128)(2,1)}, u32[]{:S(2)}) %copy-start.1) | copy-done | bytes 262168
  12.3 0.0 copy-start.2
  12.3 0.7 %copy-done.2 = s32[32,7]{0,1:T(8,128)S(1)} copy-done((s32[32,7]{0,1:T(8,128)S(1)}, s32[32,7]{0,1:T(8,128)}, u32[]{:S(2)}) %copy-start.2) | copy-done | bytes 920
  13.0 0.0 copy-start.3
  13.0 0.7 %copy-done.3 = s32[32]{0:T(128)S(1)} copy-done((s32[32]{0:T(128)S(1)}, s32[32]{0:T(128)}, u32[]{:S(2)}) %copy-start.3) | copy-done | bytes 152
  13.7 6.7 %shard_map.46 = bf16[8,32,320]{2,1,0:T(8,128)(2,1)S(1)} custom-call(s32[1]{0:T(128)} %bitcast.start_ref, s32[7,32]{1,0:T(8,128)S(1)} %bitcast.4, s32[32]{0:T(128)S(1)} %copy-done.3, bf16[32,28672]{1,0:T(8,128)(2,1)S(1)} %copy-done, bf16[32,4096]{1,0:T(8,128)(2,1)S(1)} %copy-done.1, bf16[8,4224]{1,0:T(8,128)(2,1)S(1)} %collective-permute-done.lo_ref, ...), custom_call_target="tpu_custom_call" | custom-call | tf_op jit(solution)/shard_map/pallas_call | solution.py:106
  20.3 18.3 %all_to_all.5 = bf16[8,32,320]{2,1,0:T(8,128)(2,1)S(1)} all-to-all(bf16[8,32,320]{2,1,0:T(8,128)(2,1)S(1)} %shard_map.46), channel_id=1, replica_groups=mesh['rows'=32,'cols'=8] {'cols'}, dimensions={0} | all-to-all | bytes 327680 | tf_op jit(solution)/shard_map/all_to_all | solution.py:134
  38.6 0.8 %convert.6 = f32[32,8,320]{2,1,0:T(8,128)} convert(bf16[32,8,320]{2,1,0:T(8,128)(2,1)S(1)} %bitcast.5) | non-fusion elementwise | flops 81920 | bytes 491520 | tf_op jit(solution)/shard_map/reshape | solution.py:135
  (2 shorter events, 0.0 us)
Async XLA Ops:
  1.7 8.1 %collective-permute-start = (bf16[8,4224]{1,0:T(8,128)(2,1)S(1)}, bf16[8,4224]{1,0:T(8,128)(2,1)S(1)}, u32[]{:S(2)}, u32[]{:S(2)}) collective-permute-start(bf16[8,4224]{1,0:T(8,128)(2,1)S(1)} %pad_maximum_fusion), channel_id=1, source_target_pairs={{0,1},{1,2},{2,3},{3,4},{4,5},{5,6},{6,7},{7,8},{8,9},{9,10},{10,1... | collective-permute-start | bytes 202760 | tf_op jit(solution)/shard_map/ppermute | solution.py:25
  3.5 6.4 %collective-permute-start.1 = (bf16[8,4224]{1,0:T(8,128)(2,1)S(1)}, bf16[8,4224]{1,0:T(8,128)(2,1)S(1)}, u32[]{:S(2)}, u32[]{:S(2)}) collective-permute-start(bf16[8,4224]{1,0:T(8,128)(2,1)S(1)} %pad_maximum_fusion.1), channel_id=1, source_target_pairs={{0,255},{1,0},{2,1},{3,2},{4,3},{5,4},{6,5},{7,6},{8,7},{9,8},{10,... | collective-permute-start | bytes 202760 | tf_op jit(solution)/shard_map/ppermute | solution.py:25
  9.9 1.5 %copy-start = (bf16[32,28672]{1,0:T(8,128)(2,1)S(1)}, bf16[32,28672]{1,0:T(8,128)(2,1)}, u32[]{:S(2)}) copy-start(bf16[32,28672]{1,0:T(8,128)(2,1)} %a_hbm.1) | copy-start | bytes 5505028
  11.4 0.9 %copy-start.1 = (bf16[32,4096]{1,0:T(8,128)(2,1)S(1)}, bf16[32,4096]{1,0:T(8,128)(2,1)}, u32[]{:S(2)}) copy-start(bf16[32,4096]{1,0:T(8,128)(2,1)} %p_ref.1) | copy-start | bytes 786436
  12.3 0.7 %copy-start.2 = (s32[32,7]{0,1:T(8,128)S(1)}, s32[32,7]{0,1:T(8,128)}, u32[]{:S(2)}) copy-start(s32[32,7]{0,1:T(8,128)} %param.6) | copy-start | bytes 2692
  13.0 0.7 %copy-start.3 = (s32[32]{0:T(128)S(1)}, s32[32]{0:T(128)}, u32[]{:S(2)}) copy-start(s32[32]{0:T(128)} %agg_ref.1) | copy-start | bytes 388

commit v2 on v0

v2 whole, which is shorter than its diff:
```python
import jax
import jax.numpy as jnp
from jax import lax
from jax.experimental import pallas as pl
from jax.experimental.pallas import tpu as pltpu
from jax.sharding import PartitionSpec as P

BW = 64
NS = 64
KN = 7
HW = 8
RC = 2
SL = 5
LA = 4
NB = 32
G = BW // 2
BLK = BW * BW
COLS = 8
NONE = NB
LOW = NB + 1
HIGH = LOW + HW
PLACES = HIGH + HW
INNER = tuple(range(HW, NB - HW))
OUTER = tuple(range(HW)) + tuple(range(NB - HW, NB))

VMEM = pl.BlockSpec(memory_space=pltpu.VMEM)
HBM = pl.BlockSpec(memory_space=pltpu.HBM)
SMALL = pltpu.CompilerParams(vmem_limit_bytes=24 * 1024 * 1024)


def shape(dims, dtype):
    return jax.ShapeDtypeStruct(dims, dtype)


def low_lanes(rows):
    return lax.broadcasted_iota(jnp.int32, (rows, 128), 1) < NS


def load_kernel(p_hbm, agg_hbm, cols_hbm, a_hbm, down_ref, up_ref, place_ref, agg_ref, p_ref, a_ref, agg_s, sems):
    p_in = pltpu.make_async_copy(p_hbm, p_ref, sems.at[0])
    ids_in = pltpu.make_async_copy(agg_hbm, agg_s, sems.at[1])
    cols_in = pltpu.make_async_copy(cols_hbm, place_ref, sems.at[2])
    agg_in = pltpu.make_async_copy(agg_hbm, agg_ref, sems.at[3])
    a_in = pltpu.make_async_copy(a_hbm, a_ref, sems.at[4])
    for c in (p_in, ids_in, cols_in, agg_in, a_in):
        c.start()
    ids_in.wait()
    last, first = jnp.int32(0), jnp.int32(0)
    for t in range(HW):
        last += (agg_s[NB - HW + t] == LA - 1).astype(jnp.int32)
        first += (agg_s[t] == 0).astype(jnp.int32)
    down_ref[:, BLK:] = jnp.full((HW, 128), first.astype(jnp.float32), jnp.float32).astype(jnp.bfloat16)
    up_ref[:, BLK:] = jnp.full((HW, 128), last.astype(jnp.float32), jnp.float32).astype(jnp.bfloat16)
    cols_in.wait()
    cols = place_ref[...]
    row = lax.broadcasted_iota(jnp.int32, cols.shape, 1)
    rel = row + jnp.bitwise_and(cols - row + HW, NB - 1) - HW
    place = jnp.where(rel < 0, rel + HW + LOW, jnp.where(rel < NB, rel, rel - NB + HIGH))
    place_ref[...] = jnp.where(cols < 0, NONE, place)
    p_in.wait()
    down_ref[:, :BLK] = p_ref[:HW, :]
    up_ref[:, :BLK] = p_ref[NB - HW:, :]
    agg_in.wait()
    a_in.wait()


def widen(nat, wide, low):
    even = jnp.where(low, nat, 0.0)
    odd = jnp.where(low, 0.0, nat)
    wide[pl.ds(0, G, stride=2), :] = even
    wide[pl.ds(1, G, stride=2), :] = pltpu.roll(odd, NS, 1)
    wide[pl.ds(BW, G, stride=2), :] = pltpu.roll(even, NS, 1)
    wide[pl.ds(BW + 1, G, stride=2), :] = odd


def products(rows, a_nat, w_ref, place_s, slot_of, acc):
    for k in range(KN):
        for at, i in enumerate(rows):
            block = a_nat[k, pl.ds(i, G, stride=NB), :].astype(jnp.bfloat16)
            place = place_s[k, i]
            lane = pl.multiple_of(slot_of(place, i) * 128, 128)
            acc[pl.ds(at * G, G), pl.ds(lane, 128)] += jnp.dot(block, w_ref[place], preferred_element_type=jnp.float32)


def onto_coarse(acc, sel_ref):
    return lax.dot_general(acc[...].astype(jnp.bfloat16), sel_ref[...], (((0,), (0,)), ((), ())),
                           preferred_element_type=jnp.float32)


def inner_kernel(place_v, agg_v, p_ref, a_ref, a_nat, w_ref, sel_outer, part_ref,
                 p_nat, wide, sel_inner, acc, place_s, agg_s, sems):
    place_in = pltpu.make_async_copy(place_v, place_s, sems.at[0])
    agg_in = pltpu.make_async_copy(agg_v, agg_s, sems.at[1])
    place_in.start()
    agg_in.start()
    acc[...] = jnp.zeros_like(acc)
    sel_inner[...] = jnp.zeros_like(sel_inner)
    sel_outer[...] = jnp.zeros_like(sel_outer)
    for h in range(G):
        p_nat[pl.ds(h * NB, NB), :] = p_ref[:, pl.ds(h * 128, 128)].astype(jnp.float32)
    place_in.wait()
    agg_in.wait()
    low = low_lanes(G)
    for j in range(NB):
        nat = p_nat[pl.ds(j, G, stride=NB), :]
        widen(nat, wide.at[j], low)
        w_ref[j] = wide[j].astype(jnp.bfloat16)
        lane = pl.multiple_of(agg_s[j] * 128, 128)
        if j in INNER:
            sel_inner[pl.ds(INNER.index(j) * G, G), pl.ds(lane, 128)] = nat.astype(jnp.bfloat16)
        else:
            sel_outer[pl.ds(OUTER.index(j) * G, G), pl.ds(lane, 128)] = nat.astype(jnp.bfloat16)
    w_ref[NONE] = jnp.zeros((128, 128), jnp.bfloat16)
    for k in range(KN):
        for g in range(G):
            a_nat[k, pl.ds(g * NB, NB), :] = a_ref[:, pl.ds(k * BLK + g * 128, 128)].astype(jnp.float32)

    def slot_of(place, i):
        return jnp.where(place < NB, agg_s[jnp.minimum(place, NB - 1)] - agg_s[i] + RC, RC)

    products(INNER, a_nat, w_ref, place_s, slot_of, acc)
    part_ref[...] = onto_coarse(acc, sel_inner)


def outer_kernel(place_v, agg_v, lo_ref, hi_ref, a_nat, w_own, sel_outer, part_ref, out_ref,
                 p_nat, wide, w_all, acc, y_buf, place_s, agg_s, glob, sems):
    place_in = pltpu.make_async_copy(place_v, place_s, sems.at[0])
    agg_in = pltpu.make_async_copy(agg_v, agg_s, sems.at[1])
    place_in.start()
    agg_in.start()
    below = jnp.max(lo_ref[:, BLK:].astype(jnp.float32)).astype(jnp.int32)
    above = jnp.max(hi_ref[:, BLK:].astype(jnp.float32)).astype(jnp.int32)
    acc[...] = jnp.zeros_like(acc)
    w_all[:LOW] = w_own[...]
    for h in range(G):
        lanes = pl.ds(h * 128, 128)
        p_nat[pl.ds(h * 2 * HW, HW), :] = lo_ref[:, lanes].astype(jnp.float32)
        p_nat[pl.ds(h * 2 * HW + HW, HW), :] = hi_ref[:, lanes].astype(jnp.float32)
    low = low_lanes(G)
    for j in range(2 * HW):
        widen(p_nat[pl.ds(j, G, stride=2 * HW), :], wide.at[j], low)
        w_all[LOW + j] = wide[j].astype(jnp.bfloat16)
    place_in.wait()
    agg_in.wait()
    for t in range(NB):
        glob[t] = agg_s[t]
    glob[NONE] = 1
    for t in range(HW):
        glob[LOW + t] = jnp.where(HW - t <= below, -1, -2)
        glob[HIGH + t] = jnp.where(t < above, LA, LA + 1)

    def slot_of(place, i):
        return glob[place] - agg_s[i] + RC

    products(OUTER, a_nat, w_all, place_s, slot_of, acc)
    full = part_ref[...] + onto_coarse(acc, sel_outer)
    low = low_lanes(NS)
    for c in range(LA):
        cc = full[:, c * 128:(c + 1) * 128]
        part = lambda s, par: cc[s * 128 + par * NS:s * 128 + (par + 1) * NS]
        for pair in range(3):
            s0, s1 = 2 * pair, min(2 * pair + 1, SL - 1)
            stay = jnp.where(low, part(s0, 0), part(s1, 1))
            move = jnp.where(low, part(s1, 0), part(s0, 1))
            both = stay + pltpu.roll(move, NS, 1)
            y_buf[:, pl.ds(c * 8, 8), pl.ds(pair * 128, 128)] = both.reshape(8, 8, 128)
    out_ref[...] = y_buf[:, :, :SL * NS].astype(jnp.bfloat16)


def load(prolong, aggregate, columns_t, a_blocks):
    halo = shape((HW, BLK + 128), jnp.bfloat16)
    return pl.pallas_call(
        load_kernel,
        out_shape=(halo, halo, shape((KN, NB), jnp.int32), shape((NB,), jnp.int32), shape((NB, BLK), jnp.bfloat16),
                   shape((NB, KN * BLK), jnp.bfloat16)),
        in_specs=[HBM] * 4,
        out_specs=[VMEM] * 6,
        scratch_shapes=[pltpu.SMEM((NB,), jnp.int32), pltpu.SemaphoreType.DMA((5,))],
        compiler_params=SMALL,
    )(*(pltpu.with_memory_space_constraint(x, pltpu.HBM) for x in (prolong, aggregate, columns_t, a_blocks)))


def inner(place, agg, p_v, a_v):
    n = len(INNER) * G
    return pl.pallas_call(
        inner_kernel,
        out_shape=(shape((KN, G * NB, 128), jnp.float32), shape((LOW, 128, 128), jnp.bfloat16),
                   shape((len(OUTER) * G, LA * 128), jnp.bfloat16), shape((SL * 128, LA * 128), jnp.float32)),
        in_specs=[VMEM] * 4,
        out_specs=[VMEM] * 4,
        scratch_shapes=[
            pltpu.VMEM((G * NB, 128), jnp.float32),
            pltpu.VMEM((NB, 128, 128), jnp.float32),
            pltpu.VMEM((n, LA * 128), jnp.bfloat16),
            pltpu.VMEM((n, SL * 128), jnp.float32),
            pltpu.SMEM((KN, NB), jnp.int32),
            pltpu.SMEM((NB,), jnp.int32),
            pltpu.SemaphoreType.DMA((2,)),
        ],
        compiler_params=SMALL,
    )(place, agg, p_v, a_v)


def outer(place, agg, lo, hi, a_nat, w_own, sel, part):
    return pl.pallas_call(
        outer_kernel,
        out_shape=shape((COLS, LA * NS // COLS, SL * NS), jnp.bfloat16),
        in_specs=[VMEM] * 8,
        out_specs=VMEM,
        scratch_shapes=[
            pltpu.VMEM((G * 2 * HW, 128), jnp.float32),
            pltpu.VMEM((2 * HW, 128, 128), jnp.float32),
            pltpu.VMEM((PLACES, 128, 128), jnp.bfloat16),
            pltpu.VMEM((len(OUTER) * G, SL * 128), jnp.float32),
            pltpu.VMEM((COLS, LA * NS // COLS, 3 * 128), jnp.float32),
            pltpu.SMEM((KN, NB), jnp.int32),
            pltpu.SMEM((NB,), jnp.int32),
            pltpu.SMEM((PLACES,), jnp.int32),
            pltpu.SemaphoreType.DMA((2,)),
        ],
        compiler_params=SMALL,
    )(place, agg, lo, hi, a_nat, w_own, sel, part)


def shifted(shard, by):
    axis = ("rows", "cols")
    length = lax.axis_size(axis)
    return lax.ppermute(shard, axis, [(i, (i + by) % length) for i in range(length)])


def shards(a_blocks, prolong, columns, aggregate):
    down, up, place, agg, p_v, a_v = load(prolong, aggregate, columns.T, a_blocks)
    lo = shifted(up, 1)
    hi = shifted(down, -1)
    mid = inner(place, agg, p_v, a_v)
    mine = outer(place, agg, lo, hi, *mid)
    landed = lax.all_to_all(mine, "cols", split_axis=0, concat_axis=0, tiled=True)
    return landed.astype(jnp.float32).reshape(COLS * LA, NS // COLS, SL * NS)


def solution(mesh):
    in_specs = (
        P(("rows", "cols"), None),
        P(("rows", "cols"), None),
        P(("rows", "cols"), None),
        P(("rows", "cols")),
    )
    out_specs = P("rows", "cols", None)
    return jax.shard_map(shards, mesh=mesh, in_specs=in_specs, out_specs=out_specs, check_vma=False)
```

time: 83 us -> 32.6 us (0.39)
  the two profiles are of different devices: /device:TPU:6 before, /device:TPU:31 now
where the time goes in v2:
time: 32.6 us; the launch traced here: 32.5 us
  blocking collectives  16.8 us (52%)
  Pallas kernels  8.56 us (26%)
  starting transfers between devices  6.32 us (19%)
  other arithmetic  0.77 us (2%)
    all_to_all x1, blocking collectives, shards(): lax.all_to_all(mine, 'cols', split_axis=0, concat_axis=0, tiled=True)  16.8 us
    ppermute x2, starting transfers between devices, shifted(): lax.ppermute(shard, axis, [(i, (i + by) % length) for i in range(length)])  6.32 us
    pallas_call x1, Pallas kernels, inner(): pl.pallas_call(inner_kernel, out_shape=(shape((KN, G * NB, 128), jnp.floa...  3.82 us
    pallas_call x1, Pallas kernels, outer(): pl.pallas_call(outer_kernel, out_shape=shape((COLS, LA * NS // COLS, SL *...  3.07 us
    pallas_call x1, Pallas kernels, load(): pl.pallas_call(load_kernel, out_shape=(halo, halo, shape((KN, NB), jnp.in...  1.67 us
    reshape x1, other arithmetic, shards(): return landed.astype(jnp.float32).reshape(COLS * LA, NS // COLS, SL * NS)  0.77 us
  transfers between devices with their start and end apart: 2, of which 0 were waited for; matrix products, arithmetic and copies ran while one was open for 0% of the time, Pallas kernels for 12%

profile of v2, /device:TPU:31, one launch (start us, length us, event | category | flops | bytes accessed | tf_op | source)
XLA Modules:
  0.0 32.5 jit_solution(13572612474435738225)
XLA Ops:
  0.0 1.7 %shard_map.46 = (bf16[8,4224]{1,0:T(8,128)(2,1)S(1)}, bf16[8,4224]{1,0:T(8,128)(2,1)S(1)}, s32[7,32]{1,0:T(8,128)S(1)}, s32[32]{0:T(128)S(1)}, bf16[32,4096]{1,0...) custom-call(bf16[32,4096]{1,0:T(8,128)(2,1)} %p_hbm.1, s32[32]{0:T(128)} %agg_hbm.1, s32[7,32]{1,0:T(8,128)} %bitcast.4, ...), custom_call_target="tpu_custom_call" | custom-call | tf_op jit(solution)/shard_map/pallas_call | solution.py:172
  1.7 1.7 %collective-permute-start = (bf16[8,4224]{1,0:T(8,128)(2,1)S(1)}, bf16[8,4224]{1,0:T(8,128)(2,1)S(1)}, u32[]{:S(2)}, u32[]{:S(2)}) collective-permute-start(bf16[8,4224]{1,0:T(8,128)(2,1)S(1)} %get-tuple-element.17), channel_id=1, source_target_pairs={{0,1},{1,2},{2,3},{3,4},{4,5},{5,6},{6,7},{7,8},{8,9},{9,10},{10,1... | collective-permute-start | bytes 202760 | tf_op jit(solution)/shard_map/ppermute | solution.py:228
  3.4 4.6 %collective-permute-start.1 = (bf16[8,4224]{1,0:T(8,128)(2,1)S(1)}, bf16[8,4224]{1,0:T(8,128)(2,1)S(1)}, u32[]{:S(2)}, u32[]{:S(2)}) collective-permute-start(bf16[8,4224]{1,0:T(8,128)(2,1)S(1)} %get-tuple-element.18), channel_id=1, source_target_pairs={{0,255},{1,0},{2,1},{3,2},{4,3},{5,4},{6,5},{7,6},{8,7},{9,8},{10,... | collective-permute-start | bytes 202760 | tf_op jit(solution)/shard_map/ppermute | solution.py:228
  8.0 3.8 %shard_map.47 = (f32[7,1024,128]{2,1,0:T(8,128)S(1)}, bf16[33,128,128]{2,1,0:T(8,128)(2,1)S(1)}, bf16[512,512]{1,0:T(8,128)(2,1)S(1)}, f32[640,512]{1,0:T(8,128)S(1)}) custom-call(s32[7,32]{1,0:T(8,128)S(1)} %get-tuple-element.15.place_v, s32[32]{0:T(128)S(1)} %get-tuple-element.16.agg_v, bf16[32,4096]{1,0:T(8,128)(2,1)S(1)} %get-tuple-element.19.p_ref, ...), custom_call_target="tpu_custom_call" | custom-call | tf_op jit(solution)/shard_map/pallas_call | solution.py:185
  11.8 0.0 collective-permute-done.lo_ref
  11.8 0.0 collective-permute-done.1.hi_ref
  11.9 3.1 %shard_map.48 = bf16[8,32,320]{2,1,0:T(8,128)(2,1)S(1)} custom-call(s32[7,32]{1,0:T(8,128)S(1)} %get-tuple-element.15.place_v, s32[32]{0:T(128)S(1)} %get-tuple-element.16.agg_v, bf16[8,4224]{1,0:T(8,128)(2,1)S(1)} %collective-permute-done.lo_ref, bf16[8,4224]{1,0:T(8,128)(2,1)S(1)} %collective-permute-done.1.hi_ref, ...), custom_call_target="tpu_custom_call" | custom-call | tf_op jit(solution)/shard_map/pallas_call | solution.py:205
  14.9 16.8 %all_to_all.5 = bf16[8,32,320]{2,1,0:T(8,128)(2,1)S(1)} all-to-all(bf16[8,32,320]{2,1,0:T(8,128)(2,1)S(1)} %shard_map.48), channel_id=1, replica_groups=mesh['rows'=32,'cols'=8] {'cols'}, dimensions={0} | all-to-all | bytes 327680 | tf_op jit(solution)/shard_map/all_to_all | solution.py:237
  31.7 0.8 %convert.1 = f32[32,8,320]{2,1,0:T(8,128)} convert(bf16[32,8,320]{2,1,0:T(8,128)(2,1)S(1)} %bitcast.3) | non-fusion elementwise | flops 81920 | bytes 491520 | tf_op jit(solution)/shard_map/reshape | solution.py:238
Async XLA Ops:
  1.7 10.2 %collective-permute-start = (bf16[8,4224]{1,0:T(8,128)(2,1)S(1)}, bf16[8,4224]{1,0:T(8,128)(2,1)S(1)}, u32[]{:S(2)}, u32[]{:S(2)}) collective-permute-start(bf16[8,4224]{1,0:T(8,128)(2,1)S(1)} %get-tuple-element.17), channel_id=1, source_target_pairs={{0,1},{1,2},{2,3},{3,4},{4,5},{5,6},{6,7},{7,8},{8,9},{9,10},{10,1... | collective-permute-start | bytes 202760 | tf_op jit(solution)/shard_map/ppermute | solution.py:228
  3.4 8.4 %collective-permute-start.1 = (bf16[8,4224]{1,0:T(8,128)(2,1)S(1)}, bf16[8,4224]{1,0:T(8,128)(2,1)S(1)}, u32[]{:S(2)}, u32[]{:S(2)}) collective-permute-start(bf16[8,4224]{1,0:T(8,128)(2,1)S(1)} %get-tuple-element.18), channel_id=1, source_target_pairs={{0,255},{1,0},{2,1},{3,2},{4,3},{5,4},{6,5},{7,6},{8,7},{9,8},{10,... | collective-permute-start | bytes 202760 | tf_op jit(solution)/shard_map/ppermute | solution.py:228

commit v3 on v2

v3 whole, which is shorter than its diff:
```python
import jax
import jax.numpy as jnp
from jax import lax
from jax.experimental import pallas as pl
from jax.experimental.pallas import tpu as pltpu
from jax.sharding import PartitionSpec as P

BW = 64
NS = 64
KN = 7
HW = 8
RC = 2
SL = 5
LA = 4
NB = 32
G = BW // 2
BLK = BW * BW
COLS = 8
NONE = NB
LOW = NB + 1
HIGH = LOW + HW
PLACES = HIGH + HW
STEP = NB + 8
HALO_STEP = 2 * HW + 8
IDS = ((0, 2), (0, 3), (1, 3), (2, 2))
INNER = tuple(range(HW, NB - HW))
OUTER = tuple(range(HW)) + tuple(range(NB - HW, NB))

VMEM = pl.BlockSpec(memory_space=pltpu.VMEM)
HBM = pl.BlockSpec(memory_space=pltpu.HBM)
SMALL = pltpu.CompilerParams(vmem_limit_bytes=24 * 1024 * 1024)


def shape(dims, dtype):
    return jax.ShapeDtypeStruct(dims, dtype)


def low_lanes(rows):
    return lax.broadcasted_iota(jnp.int32, (rows, 128), 1) < NS


def load_kernel(p_hbm, agg_hbm, cols_hbm, a_hbm, down_ref, up_ref, place_ref, agg_ref, p_ref, a_ref, agg_s, sems):
    p_in = pltpu.make_async_copy(p_hbm, p_ref, sems.at[0])
    ids_in = pltpu.make_async_copy(agg_hbm, agg_s, sems.at[1])
    cols_in = pltpu.make_async_copy(cols_hbm, place_ref, sems.at[2])
    agg_in = pltpu.make_async_copy(agg_hbm, agg_ref, sems.at[3])
    a_in = pltpu.make_async_copy(a_hbm, a_ref, sems.at[4])
    for c in (p_in, ids_in, cols_in, agg_in, a_in):
        c.start()
    ids_in.wait()
    last, first = jnp.int32(0), jnp.int32(0)
    for t in range(HW):
        last += (agg_s[NB - HW + t] == LA - 1).astype(jnp.int32)
        first += (agg_s[t] == 0).astype(jnp.int32)
    down_ref[:, BLK:] = jnp.full((HW, 128), first.astype(jnp.float32), jnp.float32).astype(jnp.bfloat16)
    up_ref[:, BLK:] = jnp.full((HW, 128), last.astype(jnp.float32), jnp.float32).astype(jnp.bfloat16)
    cols_in.wait()
    cols = place_ref[...]
    row = lax.broadcasted_iota(jnp.int32, cols.shape, 1)
    rel = row + jnp.bitwise_and(cols - row + HW, NB - 1) - HW
    place = jnp.where(rel < 0, rel + HW + LOW, jnp.where(rel < NB, rel, rel - NB + HIGH))
    place_ref[...] = jnp.where(cols < 0, NONE, place)
    p_in.wait()
    down_ref[:, :BLK] = p_ref[:HW, :]
    up_ref[:, :BLK] = p_ref[NB - HW:, :]
    agg_in.wait()
    a_in.wait()


def widen(nat, wide, low):
    even = jnp.where(low, nat, 0.0)
    odd = jnp.where(low, 0.0, nat)
    wide[pl.ds(0, G, stride=2), :] = even
    wide[pl.ds(1, G, stride=2), :] = pltpu.roll(odd, NS, 1)
    wide[pl.ds(BW, G, stride=2), :] = pltpu.roll(even, NS, 1)
    wide[pl.ds(BW + 1, G, stride=2), :] = odd


def products(rows, a_nat, w_ref, place_s, slot_of, accs):
    for k in range(KN):
        for i, acc in zip(rows, accs):
            block = a_nat[k, pl.ds(i, G, stride=STEP), :].astype(jnp.bfloat16)
            place = place_s[k, i]
            slot = slot_of(place, i)
            acc[slot] += jnp.dot(block, w_ref[place], preferred_element_type=jnp.float32)


def onto_coarse(groups, accs, sels):
    sums = {}
    low = low_lanes(NS)
    for at, group in enumerate(groups):
        first, count = IDS[group]
        mine = accs[at * 8:at * 8 + 8]
        rows = [jnp.concatenate([acc[s] for s in range(SL)], axis=1).astype(jnp.bfloat16) for acc in mine]
        full = lax.dot_general(jnp.concatenate(rows, axis=0), sels[at][...], (((0,), (0,)), ((), ())),
                               preferred_element_type=jnp.float32)
        for c in range(count):
            cc = full[:, c * 128:(c + 1) * 128]
            part = lambda s, par: cc[s * 128 + par * NS:s * 128 + (par + 1) * NS]
            for pair in range(3):
                s0, s1 = 2 * pair, min(2 * pair + 1, SL - 1)
                stay = jnp.where(low, part(s0, 0), part(s1, 1))
                move = jnp.where(low, part(s1, 0), part(s0, 1))
                both = stay + pltpu.roll(move, NS, 1)
                key = (first + c, pair)
                sums[key] = sums[key] + both if key in sums else both
    return sums


def inner_kernel(place_v, agg_v, p_ref, a_ref, a_nat, w_ref, sel_a, sel_d, part_ref, *scratch):
    p_nat, wide, sel_b, sel_c, place_s, agg_s, glob, sems = scratch[:8]
    accs = scratch[8:]
    place_in = pltpu.make_async_copy(place_v, place_s, sems.at[0])
    agg_in = pltpu.make_async_copy(agg_v, agg_s, sems.at[1])
    place_in.start()
    agg_in.start()
    for acc in accs:
        acc[...] = jnp.zeros_like(acc)
    sels = (sel_a, sel_b, sel_c, sel_d)
    for sel in sels:
        sel[...] = jnp.zeros_like(sel)
    for h in range(G):
        p_nat[pl.ds(h * STEP, NB), :] = p_ref[:, pl.ds(h * 128, 128)].astype(jnp.float32)
    place_in.wait()
    agg_in.wait()
    for t in range(NB):
        glob[t] = agg_s[t]
    glob[NONE] = 1
    low = low_lanes(G)
    for j in range(NB):
        nat = p_nat[pl.ds(j, G, stride=STEP), :]
        widen(nat, wide.at[j], low)
        w_ref[j] = wide[j].astype(jnp.bfloat16)
        lane = pl.multiple_of((agg_s[j] - IDS[j // 8][0]) * 128, 128)
        sels[j // 8][pl.ds(j % 8 * G, G), pl.ds(lane, 128)] = nat.astype(jnp.bfloat16)
    w_ref[NONE] = jnp.zeros((128, 128), jnp.bfloat16)
    for k in range(KN):
        for g in range(G):
            a_nat[k, pl.ds(g * STEP, NB), :] = a_ref[:, pl.ds(k * BLK + g * 128, 128)].astype(jnp.float32)

    products(INNER, a_nat, w_ref, place_s, lambda place, i: glob[place] - agg_s[i] + RC, accs)
    for (c, pair), value in onto_coarse((1, 2), accs, (sel_b, sel_c)).items():
        part_ref[:, pl.ds(c * 8, 8), pl.ds(pair * 128, 128)] = value.reshape(8, 8, 128)


def outer_kernel(place_v, agg_v, lo_ref, hi_ref, a_nat, w_own, sel_a, sel_d, part_ref, out_ref, *scratch):
    p_nat, wide, w_all, place_s, agg_s, glob, sems = scratch[:7]
    accs = scratch[7:]
    place_in = pltpu.make_async_copy(place_v, place_s, sems.at[0])
    agg_in = pltpu.make_async_copy(agg_v, agg_s, sems.at[1])
    place_in.start()
    agg_in.start()
    below = jnp.max(lo_ref[:, BLK:].astype(jnp.float32)).astype(jnp.int32)
    above = jnp.max(hi_ref[:, BLK:].astype(jnp.float32)).astype(jnp.int32)
    for acc in accs:
        acc[...] = jnp.zeros_like(acc)
    for h in range(G):
        lanes = pl.ds(h * 128, 128)
        p_nat[pl.ds(h * HALO_STEP, HW), :] = lo_ref[:, lanes].astype(jnp.float32)
        p_nat[pl.ds(h * HALO_STEP + HW, HW), :] = hi_ref[:, lanes].astype(jnp.float32)
    w_all[:LOW] = w_own[...]
    low = low_lanes(G)
    for j in range(2 * HW):
        widen(p_nat[pl.ds(j, G, stride=HALO_STEP), :], wide.at[j], low)
        w_all[LOW + j] = wide[j].astype(jnp.bfloat16)
    place_in.wait()
    agg_in.wait()
    for t in range(NB):
        glob[t] = agg_s[t]
    glob[NONE] = 1
    for t in range(HW):
        glob[LOW + t] = jnp.where(HW - t <= below, -1, -2)
        glob[HIGH + t] = jnp.where(t < above, LA, LA + 1)
    products(OUTER, a_nat, w_all, place_s, lambda place, i: glob[place] - agg_s[i] + RC, accs)
    sums = onto_coarse((0, 3), accs, (sel_a, sel_d))
    for c in range(0, LA, 2):
        for pair in range(3):
            lanes = min(128, SL * NS - pair * 128)
            both = jnp.concatenate([sums[c, pair].reshape(8, 8, 128), sums[c + 1, pair].reshape(8, 8, 128)], axis=1)
            both = both + part_ref[:, pl.ds(c * 8, 16), pl.ds(pair * 128, 128)]
            out_ref[:, pl.ds(c * 8, 16), pl.ds(pair * 128, lanes)] = both[:, :, :lanes].astype(jnp.bfloat16)


def load(prolong, aggregate, columns_t, a_blocks):
    halo = shape((HW, BLK + 128), jnp.bfloat16)
    return pl.pallas_call(
        load_kernel,
        out_shape=(halo, halo, shape((KN, NB), jnp.int32), shape((NB,), jnp.int32), shape((NB, BLK), jnp.bfloat16),
                   shape((NB, KN * BLK), jnp.bfloat16)),
        in_specs=[HBM] * 4,
        out_specs=[VMEM] * 6,
        scratch_shapes=[pltpu.SMEM((NB,), jnp.int32), pltpu.SemaphoreType.DMA((5,))],
        compiler_params=SMALL,
    )(*(pltpu.with_memory_space_constraint(x, pltpu.HBM) for x in (prolong, aggregate, columns_t, a_blocks)))


def sel_shape(group):
    return 8 * G, IDS[group][1] * 128


def inner(place, agg, p_v, a_v):
    return pl.pallas_call(
        inner_kernel,
        out_shape=(shape((KN, G * STEP, 128), jnp.float32), shape((LOW, 128, 128), jnp.bfloat16),
                   shape(sel_shape(0), jnp.bfloat16), shape(sel_shape(3), jnp.bfloat16),
                   shape((COLS, LA * NS // COLS, 3 * 128), jnp.float32)),
        in_specs=[VMEM] * 4,
        out_specs=[VMEM] * 5,
        scratch_shapes=[
            pltpu.VMEM((G * STEP, 128), jnp.float32),
            pltpu.VMEM((NB, 128, 128), jnp.float32),
            pltpu.VMEM(sel_shape(1), jnp.bfloat16),
            pltpu.VMEM(sel_shape(2), jnp.bfloat16),
            pltpu.SMEM((KN, NB), jnp.int32),
            pltpu.SMEM((NB,), jnp.int32),
            pltpu.SMEM((PLACES,), jnp.int32),
            pltpu.SemaphoreType.DMA((2,)),
        ] + [pltpu.VMEM((SL, G, 128), jnp.float32)] * len(INNER),
        compiler_params=SMALL,
    )(place, agg, p_v, a_v)


def outer(place, agg, lo, hi, *mid):
    return pl.pallas_call(
        outer_kernel,
        out_shape=shape((COLS, LA * NS // COLS, SL * NS), jnp.bfloat16),
        in_specs=[VMEM] * 9,
        out_specs=VMEM,
        scratch_shapes=[
            pltpu.VMEM((G * HALO_STEP, 128), jnp.float32),
            pltpu.VMEM((2 * HW, 128, 128), jnp.float32),
            pltpu.VMEM((PLACES, 128, 128), jnp.bfloat16),
            pltpu.SMEM((KN, NB), jnp.int32),
            pltpu.SMEM((NB,), jnp.int32),
            pltpu.SMEM((PLACES,), jnp.int32),
            pltpu.SemaphoreType.DMA((2,)),
        ] + [pltpu.VMEM((SL, G, 128), jnp.float32)] * len(OUTER),
        compiler_params=SMALL,
    )(place, agg, lo, hi, *mid)


def shifted(shard, by):
    axis = ("rows", "cols")
    length = lax.axis_size(axis)
    return lax.ppermute(shard, axis, [(i, (i + by) % length) for i in range(length)])


def shards(a_blocks, prolong, columns, aggregate):
    down, up, place, agg, p_v, a_v = load(prolong, aggregate, columns.T, a_blocks)
    lo = shifted(up, 1)
    hi = shifted(down, -1)
    mid = inner(place, agg, p_v, a_v)
    mine = outer(place, agg, lo, hi, *mid)
    landed = lax.all_to_all(mine, "cols", split_axis=0, concat_axis=0, tiled=True)
    return landed.astype(jnp.float32).reshape(COLS * LA, NS // COLS, SL * NS)


def solution(mesh):
    in_specs = (
        P(("rows", "cols"), None),
        P(("rows", "cols"), None),
        P(("rows", "cols"), None),
        P(("rows", "cols")),
    )
    out_specs = P("rows", "cols", None)
    return jax.shard_map(shards, mesh=mesh, in_specs=in_specs, out_specs=out_specs, check_vma=False)
```

time: 32.6 us -> 31 us (0.951)
  Pallas kernels: 8.56 us -> 6.63 us
    pallas_call x1, Pallas kernels: 3.82 us -> 2.83 us  [inner(): pl.pallas_call(inner_kernel, out_shape=(shape((KN, G * STEP, 128), jnp.fl...]
    pallas_call x1, Pallas kernels: 3.07 us -> 2.13 us  [outer(): pl.pallas_call(outer_kernel, out_shape=shape((COLS, LA * NS // COLS, SL *...]
    all_to_all x1, blocking collectives: 16.8 us -> 17.1 us  [shards(): lax.all_to_all(mine, 'cols', split_axis=0, concat_axis=0, tiled=True)]
  transfers between devices with their start and end apart: 2 -> 2, of which waited for: 0 -> 0; matrix products, arithmetic and copies ran while one was open for 0% -> 0% of each run, Pallas kernels for 12% -> 9%
where the time goes in v3:
time: 31 us; the launch traced here: 30.9 us
  blocking collectives  17.1 us (55%)
  Pallas kernels  6.63 us (21%)
  starting transfers between devices  6.32 us (20%)
  other arithmetic  0.77 us (2%)
    all_to_all x1, blocking collectives, shards(): lax.all_to_all(mine, 'cols', split_axis=0, concat_axis=0, tiled=True)  17.1 us
    ppermute x2, starting transfers between devices, shifted(): lax.ppermute(shard, axis, [(i, (i + by) % length) for i in range(length)])  6.32 us
    pallas_call x1, Pallas kernels, inner(): pl.pallas_call(inner_kernel, out_shape=(shape((KN, G * STEP, 128), jnp.fl...  2.83 us
    pallas_call x1, Pallas kernels, outer(): pl.pallas_call(outer_kernel, out_shape=shape((COLS, LA * NS // COLS, SL *...  2.13 us
    pallas_call x1, Pallas kernels, load(): pl.pallas_call(load_kernel, out_shape=(halo, halo, shape((KN, NB), jnp.in...  1.67 us
    reshape x1, other arithmetic, shards(): return landed.astype(jnp.float32).reshape(COLS * LA, NS // COLS, SL * NS)  0.77 us
  transfers between devices with their start and end apart: 2, of which 0 were waited for; matrix products, arithmetic and copies ran while one was open for 0% of the time, Pallas kernels for 9%

profile of v3, /device:TPU:31, one launch (start us, length us, event | category | flops | bytes accessed | tf_op | source)
XLA Modules:
  0.0 30.9 jit_solution(6219420576380641857)
XLA Ops:
  0.0 1.7 %shard_map.46 = (bf16[8,4224]{1,0:T(8,128)(2,1)S(1)}, bf16[8,4224]{1,0:T(8,128)(2,1)S(1)}, s32[7,32]{1,0:T(8,128)S(1)}, s32[32]{0:T(128)S(1)}, bf16[32,4096]{1,0...) custom-call(bf16[32,4096]{1,0:T(8,128)(2,1)} %p_hbm.1, s32[32]{0:T(128)} %agg_hbm.1, s32[7,32]{1,0:T(8,128)} %bitcast.4, ...), custom_call_target="tpu_custom_call" | custom-call | tf_op jit(solution)/shard_map/pallas_call | solution.py:186
  1.7 1.7 %collective-permute-start = (bf16[8,4224]{1,0:T(8,128)(2,1)S(1)}, bf16[8,4224]{1,0:T(8,128)(2,1)S(1)}, u32[]{:S(2)}, u32[]{:S(2)}) collective-permute-start(bf16[8,4224]{1,0:T(8,128)(2,1)S(1)} %get-tuple-element.18), channel_id=1, source_target_pairs={{0,1},{1,2},{2,3},{3,4},{4,5},{5,6},{6,7},{7,8},{8,9},{9,10},{10,1... | collective-permute-start | bytes 202760 | tf_op jit(solution)/shard_map/ppermute | solution.py:245
  3.4 4.6 %collective-permute-start.1 = (bf16[8,4224]{1,0:T(8,128)(2,1)S(1)}, bf16[8,4224]{1,0:T(8,128)(2,1)S(1)}, u32[]{:S(2)}, u32[]{:S(2)}) collective-permute-start(bf16[8,4224]{1,0:T(8,128)(2,1)S(1)} %get-tuple-element.19), channel_id=1, source_target_pairs={{0,255},{1,0},{2,1},{3,2},{4,3},{5,4},{6,5},{7,6},{8,7},{9,8},{10,... | collective-permute-start | bytes 202760 | tf_op jit(solution)/shard_map/ppermute | solution.py:245
  8.0 2.8 %shard_map.47 = (f32[7,1280,128]{2,1,0:T(8,128)S(1)}, bf16[33,128,128]{2,1,0:T(8,128)(2,1)S(1)}, bf16[256,256]{1,0:T(8,128)(2,1)S(1)}, bf16[256,256]{1,0:T(8,128)(2,1)S(1)}, f32[8,32,384]{2,1,0:T(8,128)S(1)}) custom-call(s32[7,32]{1,0:T(8,128)S(1)} %get-tuple-element.16.place_v, s32[32]{0:T(128)S(1)} %get-tuple-element.17.agg_v, ...), custom_call_target="tpu_custom_call" | custom-call | tf_op jit(solution)/shard_map/pallas_call | solution.py:202
  10.8 0.0 collective-permute-done.lo_ref
  10.9 0.0 collective-permute-done.1.hi_ref
  10.9 2.1 %shard_map.48 = bf16[8,32,320]{2,1,0:T(8,128)(2,1)S(1)} custom-call(s32[7,32]{1,0:T(8,128)S(1)} %get-tuple-element.16.place_v, s32[32]{0:T(128)S(1)} %get-tuple-element.17.agg_v, bf16[8,4224]{1,0:T(8,128)(2,1)S(1)} %collective-permute-done.lo_ref, bf16[8,4224]{1,0:T(8,128)(2,1)S(1)} %collective-permute-done.1.hi_ref, ...), custom_call_target="tpu_custom_call" | custom-call | tf_op jit(solution)/shard_map/pallas_call | solution.py:224
  13.0 17.1 %all_to_all.5 = bf16[8,32,320]{2,1,0:T(8,128)(2,1)S(1)} all-to-all(bf16[8,32,320]{2,1,0:T(8,128)(2,1)S(1)} %shard_map.48), channel_id=1, replica_groups=mesh['rows'=32,'cols'=8] {'cols'}, dimensions={0} | all-to-all | bytes 327680 | tf_op jit(solution)/shard_map/all_to_all | solution.py:254
  30.1 0.8 %convert.1 = f32[32,8,320]{2,1,0:T(8,128)} convert(bf16[32,8,320]{2,1,0:T(8,128)(2,1)S(1)} %bitcast.3) | non-fusion elementwise | flops 81920 | bytes 491520 | tf_op jit(solution)/shard_map/reshape | solution.py:255
Async XLA Ops:
  1.7 9.2 %collective-permute-start = (bf16[8,4224]{1,0:T(8,128)(2,1)S(1)}, bf16[8,4224]{1,0:T(8,128)(2,1)S(1)}, u32[]{:S(2)}, u32[]{:S(2)}) collective-permute-start(bf16[8,4224]{1,0:T(8,128)(2,1)S(1)} %get-tuple-element.18), channel_id=1, source_target_pairs={{0,1},{1,2},{2,3},{3,4},{4,5},{5,6},{6,7},{7,8},{8,9},{9,10},{10,1... | collective-permute-start | bytes 202760 | tf_op jit(solution)/shard_map/ppermute | solution.py:245
  3.4 7.5 %collective-permute-start.1 = (bf16[8,4224]{1,0:T(8,128)(2,1)S(1)}, bf16[8,4224]{1,0:T(8,128)(2,1)S(1)}, u32[]{:S(2)}, u32[]{:S(2)}) collective-permute-start(bf16[8,4224]{1,0:T(8,128)(2,1)S(1)} %get-tuple-element.19), channel_id=1, source_target_pairs={{0,255},{1,0},{2,1},{3,2},{4,3},{5,4},{6,5},{7,6},{8,7},{9,8},{10,... | collective-permute-start | bytes 202760 | tf_op jit(solution)/shard_map/ppermute | solution.py:245

commit v4 on v3

--- a/solution.py
+++ b/solution.py
@@ -247,8 +247,8 @@
 
 def shards(a_blocks, prolong, columns, aggregate):
     down, up, place, agg, p_v, a_v = load(prolong, aggregate, columns.T, a_blocks)
+    hi = shifted(down, -1)
     lo = shifted(up, 1)
-    hi = shifted(down, -1)
     mid = inner(place, agg, p_v, a_v)
     mine = outer(place, agg, lo, hi, *mid)
     landed = lax.all_to_all(mine, "cols", split_axis=0, concat_axis=0, tiled=True)

time: 31 us -> 31 us (level)
  no operation moved by 1% of the time
where the time goes in v4:
time: 31 us; the launch traced here: 30.9 us
  blocking collectives  17.1 us (55%)
  Pallas kernels  6.63 us (21%)
  starting transfers between devices  6.32 us (20%)
  other arithmetic  0.77 us (2%)
    all_to_all x1, blocking collectives, shards(): lax.all_to_all(mine, 'cols', split_axis=0, concat_axis=0, tiled=True)  17.1 us
    ppermute x2, starting transfers between devices, shifted(): lax.ppermute(shard, axis, [(i, (i + by) % length) for i in range(length)])  6.32 us
    pallas_call x1, Pallas kernels, inner(): pl.pallas_call(inner_kernel, out_shape=(shape((KN, G * STEP, 128), jnp.fl...  2.83 us
    pallas_call x1, Pallas kernels, outer(): pl.pallas_call(outer_kernel, out_shape=shape((COLS, LA * NS // COLS, SL *...  2.13 us
    pallas_call x1, Pallas kernels, load(): pl.pallas_call(load_kernel, out_shape=(halo, halo, shape((KN, NB), jnp.in...  1.67 us
    reshape x1, other arithmetic, shards(): return landed.astype(jnp.float32).reshape(COLS * LA, NS // COLS, SL * NS)  0.77 us
  transfers between devices with their start and end apart: 2, of which 0 were waited for; matrix products, arithmetic and copies ran while one was open for 0% of the time, Pallas kernels for 9%

profile of v4, /device:TPU:31, one launch (start us, length us, event | category | flops | bytes accessed | tf_op | source)
XLA Modules:
  0.0 30.9 jit_solution(6219420576380641857)
XLA Ops:
  0.0 1.7 %shard_map.46 = (bf16[8,4224]{1,0:T(8,128)(2,1)S(1)}, bf16[8,4224]{1,0:T(8,128)(2,1)S(1)}, s32[7,32]{1,0:T(8,128)S(1)}, s32[32]{0:T(128)S(1)}, bf16[32,4096]{1,0...) custom-call(bf16[32,4096]{1,0:T(8,128)(2,1)} %p_hbm.1, s32[32]{0:T(128)} %agg_hbm.1, s32[7,32]{1,0:T(8,128)} %bitcast.4, ...), custom_call_target="tpu_custom_call" | custom-call | tf_op jit(solution)/shard_map/pallas_call | solution.py:186
  1.7 1.7 %collective-permute-start = (bf16[8,4224]{1,0:T(8,128)(2,1)S(1)}, bf16[8,4224]{1,0:T(8,128)(2,1)S(1)}, u32[]{:S(2)}, u32[]{:S(2)}) collective-permute-start(bf16[8,4224]{1,0:T(8,128)(2,1)S(1)} %get-tuple-element.18), channel_id=1, source_target_pairs={{0,1},{1,2},{2,3},{3,4},{4,5},{5,6},{6,7},{7,8},{8,9},{9,10},{10,1... | collective-permute-start | bytes 202760 | tf_op jit(solution)/shard_map/ppermute | solution.py:245
  3.4 4.6 %collective-permute-start.1 = (bf16[8,4224]{1,0:T(8,128)(2,1)S(1)}, bf16[8,4224]{1,0:T(8,128)(2,1)S(1)}, u32[]{:S(2)}, u32[]{:S(2)}) collective-permute-start(bf16[8,4224]{1,0:T(8,128)(2,1)S(1)} %get-tuple-element.19), channel_id=1, source_target_pairs={{0,255},{1,0},{2,1},{3,2},{4,3},{5,4},{6,5},{7,6},{8,7},{9,8},{10,... | collective-permute-start | bytes 202760 | tf_op jit(solution)/shard_map/ppermute | solution.py:245
  8.0 2.8 %shard_map.47 = (f32[7,1280,128]{2,1,0:T(8,128)S(1)}, bf16[33,128,128]{2,1,0:T(8,128)(2,1)S(1)}, bf16[256,256]{1,0:T(8,128)(2,1)S(1)}, bf16[256,256]{1,0:T(8,128)(2,1)S(1)}, f32[8,32,384]{2,1,0:T(8,128)S(1)}) custom-call(s32[7,32]{1,0:T(8,128)S(1)} %get-tuple-element.16.place_v, s32[32]{0:T(128)S(1)} %get-tuple-element.17.agg_v, ...), custom_call_target="tpu_custom_call" | custom-call | tf_op jit(solution)/shard_map/pallas_call | solution.py:202
  10.8 0.0 collective-permute-done.lo_ref
  10.9 0.0 collective-permute-done.1.hi_ref
  10.9 2.1 %shard_map.48 = bf16[8,32,320]{2,1,0:T(8,128)(2,1)S(1)} custom-call(s32[7,32]{1,0:T(8,128)S(1)} %get-tuple-element.16.place_v, s32[32]{0:T(128)S(1)} %get-tuple-element.17.agg_v, bf16[8,4224]{1,0:T(8,128)(2,1)S(1)} %collective-permute-done.lo_ref, bf16[8,4224]{1,0:T(8,128)(2,1)S(1)} %collective-permute-done.1.hi_ref, ...), custom_call_target="tpu_custom_call" | custom-call | tf_op jit(solution)/shard_map/pallas_call | solution.py:224
  13.0 17.1 %all_to_all.5 = bf16[8,32,320]{2,1,0:T(8,128)(2,1)S(1)} all-to-all(bf16[8,32,320]{2,1,0:T(8,128)(2,1)S(1)} %shard_map.48), channel_id=1, replica_groups=mesh['rows'=32,'cols'=8] {'cols'}, dimensions={0} | all-to-all | bytes 327680 | tf_op jit(solution)/shard_map/all_to_all | solution.py:254
  30.1 0.8 %convert.1 = f32[32,8,320]{2,1,0:T(8,128)} convert(bf16[32,8,320]{2,1,0:T(8,128)(2,1)S(1)} %bitcast.3) | non-fusion elementwise | flops 81920 | bytes 491520 | tf_op jit(solution)/shard_map/reshape | solution.py:255
Async XLA Ops:
  1.7 9.2 %collective-permute-start = (bf16[8,4224]{1,0:T(8,128)(2,1)S(1)}, bf16[8,4224]{1,0:T(8,128)(2,1)S(1)}, u32[]{:S(2)}, u32[]{:S(2)}) collective-permute-start(bf16[8,4224]{1,0:T(8,128)(2,1)S(1)} %get-tuple-element.18), channel_id=1, source_target_pairs={{0,1},{1,2},{2,3},{3,4},{4,5},{5,6},{6,7},{7,8},{8,9},{9,10},{10,1... | collective-permute-start | bytes 202760 | tf_op jit(solution)/shard_map/ppermute | solution.py:245
  3.4 7.5 %collective-permute-start.1 = (bf16[8,4224]{1,0:T(8,128)(2,1)S(1)}, bf16[8,4224]{1,0:T(8,128)(2,1)S(1)}, u32[]{:S(2)}, u32[]{:S(2)}) collective-permute-start(bf16[8,4224]{1,0:T(8,128)(2,1)S(1)} %get-tuple-element.19), channel_id=1, source_target_pairs={{0,255},{1,0},{2,1},{3,2},{4,3},{5,4},{6,5},{7,6},{8,7},{9,8},{10,... | collective-permute-start | bytes 202760 | tf_op jit(solution)/shard_map/ppermute | solution.py:245

commit v5 on v4

--- a/solution.py
+++ b/solution.py
@@ -143,7 +143,7 @@
         part_ref[:, pl.ds(c * 8, 8), pl.ds(pair * 128, 128)] = value.reshape(8, 8, 128)
 
 
-def outer_kernel(place_v, agg_v, lo_ref, hi_ref, a_nat, w_own, sel_a, sel_d, part_ref, out_ref, *scratch):
+def outer_kernel(place_v, agg_v, hi_ref, lo_ref, a_nat, w_own, sel_a, sel_d, part_ref, out_ref, *scratch):
     p_nat, wide, w_all, place_s, agg_s, glob, sems = scratch[:7]
     accs = scratch[7:]
     place_in = pltpu.make_async_copy(place_v, place_s, sems.at[0])
@@ -220,7 +220,7 @@
     )(place, agg, p_v, a_v)
 
 
-def outer(place, agg, lo, hi, *mid):
+def outer(place, agg, hi, lo, *mid):
     return pl.pallas_call(
         outer_kernel,
         out_shape=shape((COLS, LA * NS // COLS, SL * NS), jnp.bfloat16),
@@ -236,7 +236,7 @@
             pltpu.SemaphoreType.DMA((2,)),
         ] + [pltpu.VMEM((SL, G, 128), jnp.float32)] * len(OUTER),
         compiler_params=SMALL,
-    )(place, agg, lo, hi, *mid)
+    )(place, agg, hi, lo, *mid)
 
 
 def shifted(shard, by):
@@ -250,7 +250,7 @@
     hi = shifted(down, -1)
     lo = shifted(up, 1)
     mid = inner(place, agg, p_v, a_v)
-    mine = outer(place, agg, lo, hi, *mid)
+    mine = outer(place, agg, hi, lo, *mid)
     landed = lax.all_to_all(mine, "cols", split_axis=0, concat_axis=0, tiled=True)
     return landed.astype(jnp.float32).reshape(COLS * LA, NS // COLS, SL * NS)
 

time: 31 us -> 34.7 us (1.12)
  the two profiles are of different devices: /device:TPU:31 before, /device:TPU:32 now
where the time goes in v5:
time: 34.7 us; the launch traced here: 34.6 us
  blocking collectives  17.6 us (51%)
  waiting for transfers between devices  7.45 us (21%)
  Pallas kernels  6.62 us (19%)
  starting transfers between devices  2.1 us (6%)
  other arithmetic  0.77 us (2%)
    all_to_all x1, blocking collectives, shards(): lax.all_to_all(mine, 'cols', split_axis=0, concat_axis=0, tiled=True)  17.6 us
    ppermute x2, waiting for transfers between devices, shifted(): lax.ppermute(shard, axis, [(i, (i + by) % length) for i in range(length)])  7.45 us
    pallas_call x1, Pallas kernels, inner(): pl.pallas_call(inner_kernel, out_shape=(shape((KN, G * STEP, 128), jnp.fl...  2.83 us
    pallas_call x1, Pallas kernels, outer(): pl.pallas_call(outer_kernel, out_shape=shape((COLS, LA * NS // COLS, SL *...  2.12 us
    ppermute x2, starting transfers between devices, shifted(): lax.ppermute(shard, axis, [(i, (i + by) % length) for i in range(length)])  2.1 us
    pallas_call x1, Pallas kernels, load(): pl.pallas_call(load_kernel, out_shape=(halo, halo, shape((KN, NB), jnp.in...  1.67 us
    reshape x1, other arithmetic, shards(): return landed.astype(jnp.float32).reshape(COLS * LA, NS // COLS, SL * NS)  0.77 us
  transfers between devices with their start and end apart: 2, of which 1 were waited for; matrix products, arithmetic and copies ran while one was open for 0% of the time, Pallas kernels for 8%

profile of v5, /device:TPU:32, one launch (start us, length us, event | category | flops | bytes accessed | tf_op | source)
XLA Modules:
  0.0 34.6 jit_solution(12240710434109799626)
XLA Ops:
  0.0 1.7 %shard_map.46 = (bf16[8,4224]{1,0:T(8,128)(2,1)S(1)}, bf16[8,4224]{1,0:T(8,128)(2,1)S(1)}, s32[7,32]{1,0:T(8,128)S(1)}, s32[32]{0:T(128)S(1)}, bf16[32,4096]{1,0...) custom-call(bf16[32,4096]{1,0:T(8,128)(2,1)} %p_hbm.1, s32[32]{0:T(128)} %agg_hbm.1, s32[7,32]{1,0:T(8,128)} %bitcast.4, ...), custom_call_target="tpu_custom_call" | custom-call | tf_op jit(solution)/shard_map/pallas_call | solution.py:186
  1.7 1.9 %collective-permute-start = (bf16[8,4224]{1,0:T(8,128)(2,1)S(1)}, bf16[8,4224]{1,0:T(8,128)(2,1)S(1)}, u32[]{:S(2)}, u32[]{:S(2)}) collective-permute-start(bf16[8,4224]{1,0:T(8,128)(2,1)S(1)} %get-tuple-element.18), channel_id=1, source_target_pairs={{0,255},{1,0},{2,1},{3,2},{4,3},{5,4},{6,5},{7,6},{8,7},{9,8},{10,... | collective-permute-start | bytes 202760 | tf_op jit(solution)/shard_map/ppermute | solution.py:245
  3.6 0.2 collective-permute-start.1
  3.8 2.8 %shard_map.47 = (f32[7,1280,128]{2,1,0:T(8,128)S(1)}, bf16[33,128,128]{2,1,0:T(8,128)(2,1)S(1)}, bf16[256,256]{1,0:T(8,128)(2,1)S(1)}, bf16[256,256]{1,0:T(8,128)(2,1)S(1)}, f32[8,32,384]{2,1,0:T(8,128)S(1)}) custom-call(s32[7,32]{1,0:T(8,128)S(1)} %get-tuple-element.16.place_v, s32[32]{0:T(128)S(1)} %get-tuple-element.17.agg_v, ...), custom_call_target="tpu_custom_call" | custom-call | tf_op jit(solution)/shard_map/pallas_call | solution.py:202
  6.6 0.0 collective-permute-done.hi_ref
  6.6 7.5 %collective-permute-done.1.lo_ref = bf16[8,4224]{1,0:T(8,128)(2,1)S(1)} collective-permute-done((bf16[8,4224]{1,0:T(8,128)(2,1)S(1)}, bf16[8,4224]{1,0:T(8,128)(2,1)S(1)}, u32[]{:S(2)}, u32[]{:S(2)}) %collective-permute-start.1) | collective-permute-done | bytes 67616 | tf_op jit(solution)/shard_map/ppermute | solution.py:245
  14.1 2.1 %shard_map.48 = bf16[8,32,320]{2,1,0:T(8,128)(2,1)S(1)} custom-call(s32[7,32]{1,0:T(8,128)S(1)} %get-tuple-element.16.place_v, s32[32]{0:T(128)S(1)} %get-tuple-element.17.agg_v, bf16[8,4224]{1,0:T(8,128)(2,1)S(1)} %collective-permute-done.hi_ref, bf16[8,4224]{1,0:T(8,128)(2,1)S(1)} %collective-permute-done.1.lo_ref, ...), custom_call_target="tpu_custom_call" | custom-call | tf_op jit(solution)/shard_map/pallas_call | solution.py:224
  16.2 17.6 %all_to_all.5 = bf16[8,32,320]{2,1,0:T(8,128)(2,1)S(1)} all-to-all(bf16[8,32,320]{2,1,0:T(8,128)(2,1)S(1)} %shard_map.48), channel_id=1, replica_groups=mesh['rows'=32,'cols'=8] {'cols'}, dimensions={0} | all-to-all | bytes 327680 | tf_op jit(solution)/shard_map/all_to_all | solution.py:254
  33.8 0.8 %convert.1 = f32[32,8,320]{2,1,0:T(8,128)} convert(bf16[32,8,320]{2,1,0:T(8,128)(2,1)S(1)} %bitcast.3) | non-fusion elementwise | flops 81920 | bytes 491520 | tf_op jit(solution)/shard_map/reshape | solution.py:255
Async XLA Ops:
  1.7 4.9 %collective-permute-start = (bf16[8,4224]{1,0:T(8,128)(2,1)S(1)}, bf16[8,4224]{1,0:T(8,128)(2,1)S(1)}, u32[]{:S(2)}, u32[]{:S(2)}) collective-permute-start(bf16[8,4224]{1,0:T(8,128)(2,1)S(1)} %get-tuple-element.18), channel_id=1, source_target_pairs={{0,255},{1,0},{2,1},{3,2},{4,3},{5,4},{6,5},{7,6},{8,7},{9,8},{10,... | collective-permute-start | bytes 202760 | tf_op jit(solution)/shard_map/ppermute | solution.py:245
  3.6 10.5 %collective-permute-start.1 = (bf16[8,4224]{1,0:T(8,128)(2,1)S(1)}, bf16[8,4224]{1,0:T(8,128)(2,1)S(1)}, u32[]{:S(2)}, u32[]{:S(2)}) collective-permute-start(bf16[8,4224]{1,0:T(8,128)(2,1)S(1)} %get-tuple-element.19), channel_id=1, source_target_pairs={{0,1},{1,2},{2,3},{3,4},{4,5},{5,6},{6,7},{7,8},{8,9},{9,10},{10,1... | collective-permute-start | bytes 202760 | tf_op jit(solution)/shard_map/ppermute | solution.py:245

commit v6 on v5

--- a/solution.py
+++ b/solution.py
@@ -39,7 +39,11 @@
     return lax.broadcasted_iota(jnp.int32, (rows, 128), 1) < NS
 
 
-def load_kernel(p_hbm, agg_hbm, cols_hbm, a_hbm, down_ref, up_ref, place_ref, agg_ref, p_ref, a_ref, agg_s, sems):
+def is_even():
+    return jnp.bitwise_and(lax.axis_index("cols"), 1) == 0
+
+
+def load_kernel(p_hbm, agg_hbm, cols_hbm, a_hbm, first_ref, second_ref, place_ref, agg_ref, p_ref, a_ref, agg_s, sems):
     p_in = pltpu.make_async_copy(p_hbm, p_ref, sems.at[0])
     ids_in = pltpu.make_async_copy(agg_hbm, agg_s, sems.at[1])
     cols_in = pltpu.make_async_copy(cols_hbm, place_ref, sems.at[2])
@@ -52,8 +56,6 @@
     for t in range(HW):
         last += (agg_s[NB - HW + t] == LA - 1).astype(jnp.int32)
         first += (agg_s[t] == 0).astype(jnp.int32)
-    down_ref[:, BLK:] = jnp.full((HW, 128), first.astype(jnp.float32), jnp.float32).astype(jnp.bfloat16)
-    up_ref[:, BLK:] = jnp.full((HW, 128), last.astype(jnp.float32), jnp.float32).astype(jnp.bfloat16)
     cols_in.wait()
     cols = place_ref[...]
     row = lax.broadcasted_iota(jnp.int32, cols.shape, 1)
@@ -61,8 +63,16 @@
     place = jnp.where(rel < 0, rel + HW + LOW, jnp.where(rel < NB, rel, rel - NB + HIGH))
     place_ref[...] = jnp.where(cols < 0, NONE, place)
     p_in.wait()
-    down_ref[:, :BLK] = p_ref[:HW, :]
-    up_ref[:, :BLK] = p_ref[NB - HW:, :]
+    even = is_even()
+
+    def fill(up_ref, down_ref):
+        up_ref[:, :BLK] = p_ref[NB - HW:, :]
+        up_ref[:, BLK:] = jnp.full((HW, 128), last.astype(jnp.float32), jnp.float32).astype(jnp.bfloat16)
+        down_ref[:, :BLK] = p_ref[:HW, :]
+        down_ref[:, BLK:] = jnp.full((HW, 128), first.astype(jnp.float32), jnp.float32).astype(jnp.bfloat16)
+
+    pl.when(even)(lambda: fill(first_ref, second_ref))
+    pl.when(jnp.logical_not(even))(lambda: fill(second_ref, first_ref))
     agg_in.wait()
     a_in.wait()
 
@@ -143,21 +153,26 @@
         part_ref[:, pl.ds(c * 8, 8), pl.ds(pair * 128, 128)] = value.reshape(8, 8, 128)
 
 
-def outer_kernel(place_v, agg_v, hi_ref, lo_ref, a_nat, w_own, sel_a, sel_d, part_ref, out_ref, *scratch):
+def outer_kernel(place_v, agg_v, first_ref, second_ref, a_nat, w_own, sel_a, sel_d, part_ref, out_ref, *scratch):
     p_nat, wide, w_all, place_s, agg_s, glob, sems = scratch[:7]
     accs = scratch[7:]
     place_in = pltpu.make_async_copy(place_v, place_s, sems.at[0])
     agg_in = pltpu.make_async_copy(agg_v, agg_s, sems.at[1])
     place_in.start()
     agg_in.start()
-    below = jnp.max(lo_ref[:, BLK:].astype(jnp.float32)).astype(jnp.int32)
-    above = jnp.max(hi_ref[:, BLK:].astype(jnp.float32)).astype(jnp.int32)
+    even = is_even()
+    in_first = jnp.max(first_ref[:, BLK:].astype(jnp.float32)).astype(jnp.int32)
+    in_second = jnp.max(second_ref[:, BLK:].astype(jnp.float32)).astype(jnp.int32)
+    below = jnp.where(even, in_second, in_first)
+    above = jnp.where(even, in_first, in_second)
+    at_first = pl.multiple_of(jnp.where(even, HW, 0), HW)
+    at_second = pl.multiple_of(jnp.where(even, 0, HW), HW)
     for acc in accs:
         acc[...] = jnp.zeros_like(acc)
     for h in range(G):
         lanes = pl.ds(h * 128, 128)
-        p_nat[pl.ds(h * HALO_STEP, HW), :] = lo_ref[:, lanes].astype(jnp.float32)
-        p_nat[pl.ds(h * HALO_STEP + HW, HW), :] = hi_ref[:, lanes].astype(jnp.float32)
+        p_nat[pl.ds(h * HALO_STEP + at_first, HW), :] = first_ref[:, lanes].astype(jnp.float32)
+        p_nat[pl.ds(h * HALO_STEP + at_second, HW), :] = second_ref[:, lanes].astype(jnp.float32)
     w_all[:LOW] = w_own[...]
     low = low_lanes(G)
     for j in range(2 * HW):
@@ -220,7 +235,7 @@
     )(place, agg, p_v, a_v)
 
 
-def outer(place, agg, hi, lo, *mid):
+def outer(place, agg, first, second, *mid):
     return pl.pallas_call(
         outer_kernel,
         out_shape=shape((COLS, LA * NS // COLS, SL * NS), jnp.bfloat16),
@@ -236,21 +251,22 @@
             pltpu.SemaphoreType.DMA((2,)),
         ] + [pltpu.VMEM((SL, G, 128), jnp.float32)] * len(OUTER),
         compiler_params=SMALL,
-    )(place, agg, hi, lo, *mid)
-
-
-def shifted(shard, by):
+    )(place, agg, first, second, *mid)
+
+
+def exchanged(shard, first):
     axis = ("rows", "cols")
     length = lax.axis_size(axis)
-    return lax.ppermute(shard, axis, [(i, (i + by) % length) for i in range(length)])
+    pairs = [(i, (i + (1 if (i % 2 == 0) == first else -1)) % length) for i in range(length)]
+    return lax.ppermute(shard, axis, pairs)
 
 
 def shards(a_blocks, prolong, columns, aggregate):
-    down, up, place, agg, p_v, a_v = load(prolong, aggregate, columns.T, a_blocks)
-    hi = shifted(down, -1)
-    lo = shifted(up, 1)
+    first, second, place, agg, p_v, a_v = load(prolong, aggregate, columns.T, a_blocks)
+    first = exchanged(first, True)
+    second = exchanged(second, False)
     mid = inner(place, agg, p_v, a_v)
-    mine = outer(place, agg, hi, lo, *mid)
+    mine = outer(place, agg, first, second, *mid)
     landed = lax.all_to_all(mine, "cols", split_axis=0, concat_axis=0, tiled=True)
     return landed.astype(jnp.float32).reshape(COLS * LA, NS // COLS, SL * NS)
 

time: 34.7 us -> 31.5 us (0.908)
  the two profiles are of different devices: /device:TPU:32 before, /device:TPU:31 now
where the time goes in v6:
time: 31.5 us; the launch traced here: 31.3 us
  blocking collectives  16.6 us (53%)
  starting transfers between devices  7.23 us (23%)
  Pallas kernels  6.63 us (21%)
  other arithmetic  0.77 us (2%)
    all_to_all x1, blocking collectives, shards(): lax.all_to_all(mine, 'cols', split_axis=0, concat_axis=0, tiled=True)  16.6 us
    ppermute x2, starting transfers between devices, exchanged(): return lax.ppermute(shard, axis, pairs)  7.23 us
    pallas_call x1, Pallas kernels, inner(): pl.pallas_call(inner_kernel, out_shape=(shape((KN, G * STEP, 128), jnp.fl...  2.83 us
    pallas_call x1, Pallas kernels, outer(): pl.pallas_call(outer_kernel, out_shape=shape((COLS, LA * NS // COLS, SL *...  2.13 us
    pallas_call x1, Pallas kernels, load(): pl.pallas_call(load_kernel, out_shape=(halo, halo, shape((KN, NB), jnp.in...  1.67 us
    reshape x1, other arithmetic, shards(): return landed.astype(jnp.float32).reshape(COLS * LA, NS // COLS, SL * NS)  0.77 us
  transfers between devices with their start and end apart: 2, of which 0 were waited for; matrix products, arithmetic and copies ran while one was open for 0% of the time, Pallas kernels for 9%

profile of v6, /device:TPU:31, one launch (start us, length us, event | category | flops | bytes accessed | tf_op | source)
XLA Modules:
  0.0 31.3 jit_solution(15017896058628988205)
XLA Ops:
  0.0 1.7 %shard_map.46 = (bf16[8,4224]{1,0:T(8,128)(2,1)S(1)}, bf16[8,4224]{1,0:T(8,128)(2,1)S(1)}, s32[7,32]{1,0:T(8,128)S(1)}, s32[32]{0:T(128)S(1)}, bf16[32,4096]{1,0...) custom-call(bf16[32,4096]{1,0:T(8,128)(2,1)} %p_hbm.1, s32[32]{0:T(128)} %agg_hbm.1, s32[7,32]{1,0:T(8,128)} %bitcast.4, ...), custom_call_target="tpu_custom_call" | custom-call | tf_op jit(solution)/shard_map/pallas_call | solution.py:201
  1.7 1.7 %collective-permute-start = (bf16[8,4224]{1,0:T(8,128)(2,1)S(1)}, bf16[8,4224]{1,0:T(8,128)(2,1)S(1)}, u32[]{:S(2)}, u32[]{:S(2)}) collective-permute-start(bf16[8,4224]{1,0:T(8,128)(2,1)S(1)} %get-tuple-element.18), channel_id=1, source_target_pairs={{0,1},{1,0},{2,3},{3,2},{4,5},{5,4},{6,7},{7,6},{8,9},{9,8},{10,11... | collective-permute-start | bytes 202760 | tf_op jit(solution)/shard_map/ppermute | solution.py:261
  3.4 5.5 %collective-permute-start.1 = (bf16[8,4224]{1,0:T(8,128)(2,1)S(1)}, bf16[8,4224]{1,0:T(8,128)(2,1)S(1)}, u32[]{:S(2)}, u32[]{:S(2)}) collective-permute-start(bf16[8,4224]{1,0:T(8,128)(2,1)S(1)} %get-tuple-element.19), channel_id=1, source_target_pairs={{0,255},{1,2},{2,1},{3,4},{4,3},{5,6},{6,5},{7,8},{8,7},{9,10},{10... | collective-permute-start | bytes 202760 | tf_op jit(solution)/shard_map/ppermute | solution.py:261
  8.9 2.8 %shard_map.47 = (f32[7,1280,128]{2,1,0:T(8,128)S(1)}, bf16[33,128,128]{2,1,0:T(8,128)(2,1)S(1)}, bf16[256,256]{1,0:T(8,128)(2,1)S(1)}, bf16[256,256]{1,0:T(8,128)(2,1)S(1)}, f32[8,32,384]{2,1,0:T(8,128)S(1)}) custom-call(s32[7,32]{1,0:T(8,128)S(1)} %get-tuple-element.16.place_v, s32[32]{0:T(128)S(1)} %get-tuple-element.17.agg_v, ...), custom_call_target="tpu_custom_call" | custom-call | tf_op jit(solution)/shard_map/pallas_call | solution.py:217
  11.7 0.0 collective-permute-done.first_ref
  11.8 0.0 collective-permute-done.1.second_ref
  11.8 2.1 %shard_map.48 = bf16[8,32,320]{2,1,0:T(8,128)(2,1)S(1)} custom-call(s32[7,32]{1,0:T(8,128)S(1)} %get-tuple-element.16.place_v, s32[32]{0:T(128)S(1)} %get-tuple-element.17.agg_v, bf16[8,4224]{1,0:T(8,128)(2,1)S(1)} %collective-permute-done.first_ref, bf16[8,4224]{1,0:T(8,128)(2,1)S(1)} %collective-permute-done.1.second_ref, ...), custom_call_target="tpu_custom_call" | custom-call | tf_op jit(solution)/shard_map/pallas_call | solution.py:239
  13.9 16.6 %all_to_all.5 = bf16[8,32,320]{2,1,0:T(8,128)(2,1)S(1)} all-to-all(bf16[8,32,320]{2,1,0:T(8,128)(2,1)S(1)} %shard_map.48), channel_id=1, replica_groups=mesh['rows'=32,'cols'=8] {'cols'}, dimensions={0} | all-to-all | bytes 327680 | tf_op jit(solution)/shard_map/all_to_all | solution.py:270
  30.6 0.8 %convert.1 = f32[32,8,320]{2,1,0:T(8,128)} convert(bf16[32,8,320]{2,1,0:T(8,128)(2,1)S(1)} %bitcast.3) | non-fusion elementwise | flops 81920 | bytes 491520 | tf_op jit(solution)/shard_map/reshape | solution.py:271
Async XLA Ops:
  1.7 10.1 %collective-permute-start = (bf16[8,4224]{1,0:T(8,128)(2,1)S(1)}, bf16[8,4224]{1,0:T(8,128)(2,1)S(1)}, u32[]{:S(2)}, u32[]{:S(2)}) collective-permute-start(bf16[8,4224]{1,0:T(8,128)(2,1)S(1)} %get-tuple-element.18), channel_id=1, source_target_pairs={{0,1},{1,0},{2,3},{3,2},{4,5},{5,4},{6,7},{7,6},{8,9},{9,8},{10,11... | collective-permute-start | bytes 202760 | tf_op jit(solution)/shard_map/ppermute | solution.py:261
  3.4 8.4 %collective-permute-start.1 = (bf16[8,4224]{1,0:T(8,128)(2,1)S(1)}, bf16[8,4224]{1,0:T(8,128)(2,1)S(1)}, u32[]{:S(2)}, u32[]{:S(2)}) collective-permute-start(bf16[8,4224]{1,0:T(8,128)(2,1)S(1)} %get-tuple-element.19), channel_id=1, source_target_pairs={{0,255},{1,2},{2,1},{3,4},{4,3},{5,6},{6,5},{7,8},{8,7},{9,10},{10... | collective-permute-start | bytes 202760 | tf_op jit(solution)/shard_map/ppermute | solution.py:261

commit v7 on v6

--- a/solution.py
+++ b/solution.py
@@ -39,17 +39,16 @@
     return lax.broadcasted_iota(jnp.int32, (rows, 128), 1) < NS
 
 
-def is_even():
-    return jnp.bitwise_and(lax.axis_index("cols"), 1) == 0
-
-
-def load_kernel(p_hbm, agg_hbm, cols_hbm, a_hbm, first_ref, second_ref, place_ref, agg_ref, p_ref, a_ref, agg_s, sems):
+def above_first():
+    return jnp.bitwise_and(lax.axis_index("cols"), 1) == 1
+
+
+def load_kernel(p_hbm, agg_hbm, cols_hbm, first_ref, second_ref, place_ref, agg_ref, p_ref, agg_s, sems):
     p_in = pltpu.make_async_copy(p_hbm, p_ref, sems.at[0])
     ids_in = pltpu.make_async_copy(agg_hbm, agg_s, sems.at[1])
     cols_in = pltpu.make_async_copy(cols_hbm, place_ref, sems.at[2])
     agg_in = pltpu.make_async_copy(agg_hbm, agg_ref, sems.at[3])
-    a_in = pltpu.make_async_copy(a_hbm, a_ref, sems.at[4])
-    for c in (p_in, ids_in, cols_in, agg_in, a_in):
+    for c in (p_in, ids_in, cols_in, agg_in):
         c.start()
     ids_in.wait()
     last, first = jnp.int32(0), jnp.int32(0)
@@ -63,7 +62,7 @@
     place = jnp.where(rel < 0, rel + HW + LOW, jnp.where(rel < NB, rel, rel - NB + HIGH))
     place_ref[...] = jnp.where(cols < 0, NONE, place)
     p_in.wait()
-    even = is_even()
+    up_first = above_first()
 
     def fill(up_ref, down_ref):
         up_ref[:, :BLK] = p_ref[NB - HW:, :]
@@ -71,10 +70,9 @@
         down_ref[:, :BLK] = p_ref[:HW, :]
         down_ref[:, BLK:] = jnp.full((HW, 128), first.astype(jnp.float32), jnp.float32).astype(jnp.bfloat16)
 
-    pl.when(even)(lambda: fill(first_ref, second_ref))
-    pl.when(jnp.logical_not(even))(lambda: fill(second_ref, first_ref))
+    pl.when(up_first)(lambda: fill(first_ref, second_ref))
+    pl.when(jnp.logical_not(up_first))(lambda: fill(second_ref, first_ref))
     agg_in.wait()
-    a_in.wait()
 
 
 def widen(nat, wide, low):
@@ -117,9 +115,14 @@
     return sums
 
 
-def inner_kernel(place_v, agg_v, p_ref, a_ref, a_nat, w_ref, sel_a, sel_d, part_ref, *scratch):
-    p_nat, wide, sel_b, sel_c, place_s, agg_s, glob, sems = scratch[:8]
-    accs = scratch[8:]
+def inner_kernel(place_v, agg_v, p_ref, a_hbm, a_nat, w_ref, sel_a, sel_d, part_ref, *scratch):
+    a_ref, p_nat, wide, sel_b, sel_c, place_s, agg_s, glob, sems = scratch[:9]
+    accs = scratch[9:]
+    a_in = []
+    for k in range(KN):
+        part = (slice(None), pl.ds(k * BLK, BLK))
+        a_in.append(pltpu.make_async_copy(a_hbm.at[part], a_ref.at[part], sems.at[2 + k]))
+        a_in[k].start()
     place_in = pltpu.make_async_copy(place_v, place_s, sems.at[0])
     agg_in = pltpu.make_async_copy(agg_v, agg_s, sems.at[1])
     place_in.start()
@@ -145,6 +148,7 @@
         sels[j // 8][pl.ds(j % 8 * G, G), pl.ds(lane, 128)] = nat.astype(jnp.bfloat16)
     w_ref[NONE] = jnp.zeros((128, 128), jnp.bfloat16)
     for k in range(KN):
+        a_in[k].wait()
         for g in range(G):
             a_nat[k, pl.ds(g * STEP, NB), :] = a_ref[:, pl.ds(k * BLK + g * 128, 128)].astype(jnp.float32)
 
@@ -160,13 +164,13 @@
     agg_in = pltpu.make_async_copy(agg_v, agg_s, sems.at[1])
     place_in.start()
     agg_in.start()
-    even = is_even()
+    up_first = above_first()
     in_first = jnp.max(first_ref[:, BLK:].astype(jnp.float32)).astype(jnp.int32)
     in_second = jnp.max(second_ref[:, BLK:].astype(jnp.float32)).astype(jnp.int32)
-    below = jnp.where(even, in_second, in_first)
-    above = jnp.where(even, in_first, in_second)
-    at_first = pl.multiple_of(jnp.where(even, HW, 0), HW)
-    at_second = pl.multiple_of(jnp.where(even, 0, HW), HW)
+    below = jnp.where(up_first, in_second, in_first)
+    above = jnp.where(up_first, in_first, in_second)
+    at_first = pl.multiple_of(jnp.where(up_first, HW, 0), HW)
+    at_second = pl.multiple_of(jnp.where(up_first, 0, HW), HW)
     for acc in accs:
         acc[...] = jnp.zeros_like(acc)
     for h in range(G):
@@ -196,32 +200,32 @@
             out_ref[:, pl.ds(c * 8, 16), pl.ds(pair * 128, lanes)] = both[:, :, :lanes].astype(jnp.bfloat16)
 
 
-def load(prolong, aggregate, columns_t, a_blocks):
+def load(prolong, aggregate, columns_t):
     halo = shape((HW, BLK + 128), jnp.bfloat16)
     return pl.pallas_call(
         load_kernel,
-        out_shape=(halo, halo, shape((KN, NB), jnp.int32), shape((NB,), jnp.int32), shape((NB, BLK), jnp.bfloat16),
-                   shape((NB, KN * BLK), jnp.bfloat16)),
-        in_specs=[HBM] * 4,
-        out_specs=[VMEM] * 6,
-        scratch_shapes=[pltpu.SMEM((NB,), jnp.int32), pltpu.SemaphoreType.DMA((5,))],
+        out_shape=(halo, halo, shape((KN, NB), jnp.int32), shape((NB,), jnp.int32), shape((NB, BLK), jnp.bfloat16)),
+        in_specs=[HBM] * 3,
+        out_specs=[VMEM] * 5,
+        scratch_shapes=[pltpu.SMEM((NB,), jnp.int32), pltpu.SemaphoreType.DMA((4,))],
         compiler_params=SMALL,
-    )(*(pltpu.with_memory_space_constraint(x, pltpu.HBM) for x in (prolong, aggregate, columns_t, a_blocks)))
+    )(*(pltpu.with_memory_space_constraint(x, pltpu.HBM) for x in (prolong, aggregate, columns_t)))
 
 
 def sel_shape(group):
     return 8 * G, IDS[group][1] * 128
 
 
-def inner(place, agg, p_v, a_v):
+def inner(place, agg, p_v, a_blocks):
     return pl.pallas_call(
         inner_kernel,
         out_shape=(shape((KN, G * STEP, 128), jnp.float32), shape((LOW, 128, 128), jnp.bfloat16),
                    shape(sel_shape(0), jnp.bfloat16), shape(sel_shape(3), jnp.bfloat16),
                    shape((COLS, LA * NS // COLS, 3 * 128), jnp.float32)),
-        in_specs=[VMEM] * 4,
+        in_specs=[VMEM] * 3 + [HBM],
         out_specs=[VMEM] * 5,
         scratch_shapes=[
+            pltpu.VMEM((NB, KN * BLK), jnp.bfloat16),
             pltpu.VMEM((G * STEP, 128), jnp.float32),
             pltpu.VMEM((NB, 128, 128), jnp.float32),
             pltpu.VMEM(sel_shape(1), jnp.bfloat16),
@@ -229,10 +233,10 @@
             pltpu.SMEM((KN, NB), jnp.int32),
             pltpu.SMEM((NB,), jnp.int32),
             pltpu.SMEM((PLACES,), jnp.int32),
-            pltpu.SemaphoreType.DMA((2,)),
+            pltpu.SemaphoreType.DMA((2 + KN,)),
         ] + [pltpu.VMEM((SL, G, 128), jnp.float32)] * len(INNER),
         compiler_params=SMALL,
-    )(place, agg, p_v, a_v)
+    )(place, agg, p_v, pltpu.with_memory_space_constraint(a_blocks, pltpu.HBM))
 
 
 def outer(place, agg, first, second, *mid):
@@ -257,15 +261,15 @@
 def exchanged(shard, first):
     axis = ("rows", "cols")
     length = lax.axis_size(axis)
-    pairs = [(i, (i + (1 if (i % 2 == 0) == first else -1)) % length) for i in range(length)]
+    pairs = [(i, (i + (1 if (i % 2 == 1) == first else -1)) % length) for i in range(length)]
     return lax.ppermute(shard, axis, pairs)
 
 
 def shards(a_blocks, prolong, columns, aggregate):
-    first, second, place, agg, p_v, a_v = load(prolong, aggregate, columns.T, a_blocks)
+    first, second, place, agg, p_v = load(prolong, aggregate, columns.T)
     first = exchanged(first, True)
     second = exchanged(second, False)
-    mid = inner(place, agg, p_v, a_v)
+    mid = inner(place, agg, p_v, a_blocks)
     mine = outer(place, agg, first, second, *mid)
     landed = lax.all_to_all(mine, "cols", split_axis=0, concat_axis=0, tiled=True)
     return landed.astype(jnp.float32).reshape(COLS * LA, NS // COLS, SL * NS)

time: 31.5 us -> 29.8 us (0.946)
  starting transfers between devices: 7.23 us -> 6.23 us
  blocking collectives: 16.6 us -> 15.8 us
  waiting for transfers between devices: 0.01 us -> 0.55 us
  Pallas kernels: 6.63 us -> 6.26 us
    ppermute x2, starting transfers between devices: 7.23 us -> 6.23 us  [exchanged(): return lax.ppermute(shard, axis, pairs)]
    all_to_all x1, blocking collectives: 16.6 us -> 15.8 us  [shards(): lax.all_to_all(mine, 'cols', split_axis=0, concat_axis=0, tiled=True)]
    pallas_call x1, Pallas kernels: 1.67 us -> 1 us  [load(): pl.pallas_call(load_kernel, out_shape=(halo, halo, shape((KN, NB), jnp.in...]
    ppermute x2, waiting for transfers between devices: 0.01 us -> 0.55 us  [exchanged(): return lax.ppermute(shard, axis, pairs)]
  transfers between devices with their start and end apart: 2 -> 2, of which waited for: 0 -> 1; matrix products, arithmetic and copies ran while one was open for 0% -> 0% of each run, Pallas kernels for 9% -> 11%
where the time goes in v7:
time: 29.8 us; the launch traced here: 29.6 us
  blocking collectives  15.8 us (53%)
  Pallas kernels  6.26 us (21%)
  starting transfers between devices  6.23 us (21%)
  other arithmetic  0.77 us (3%)
  waiting for transfers between devices  0.55 us (2%)
    all_to_all x1, blocking collectives, shards(): lax.all_to_all(mine, 'cols', split_axis=0, concat_axis=0, tiled=True)  15.8 us
    ppermute x2, starting transfers between devices, exchanged(): return lax.ppermute(shard, axis, pairs)  6.23 us
    pallas_call x1, Pallas kernels, inner(): pl.pallas_call(inner_kernel, out_shape=(shape((KN, G * STEP, 128), jnp.fl...  3.13 us
    pallas_call x1, Pallas kernels, outer(): pl.pallas_call(outer_kernel, out_shape=shape((COLS, LA * NS // COLS, SL *...  2.13 us
    pallas_call x1, Pallas kernels, load(): pl.pallas_call(load_kernel, out_shape=(halo, halo, shape((KN, NB), jnp.in...  1 us
    reshape x1, other arithmetic, shards(): return landed.astype(jnp.float32).reshape(COLS * LA, NS // COLS, SL * NS)  0.77 us
  transfers between devices with their start and end apart: 2, of which 1 were waited for; matrix products, arithmetic and copies ran while one was open for 0% of the time, Pallas kernels for 11%

profile of v7, /device:TPU:31, one launch (start us, length us, event | category | flops | bytes accessed | tf_op | source)
XLA Modules:
  0.0 29.6 jit_solution(16523048908743062569)
XLA Ops:
  0.0 1.0 %shard_map.46 = (bf16[8,4224]{1,0:T(8,128)(2,1)S(1)}, bf16[8,4224]{1,0:T(8,128)(2,1)S(1)}, s32[7,32]{1,0:T(8,128)S(1)}, s32[32]{0:T(128)S(1)}, bf16[32,4096]{1,0:T(8,128)(2,1)S(1)}) custom-call(bf16[32,4096]{1,0:T(8,128)(2,1)} %p_hbm.1, s32[32]{0:T(128)} %agg_hbm.1, s32[7,32]{1,0:T(8,128)} %bitcast.4), custom_call_target="tpu_custom_call" | custom-call | tf_op jit(solution)/shard_map/pallas_call | solution.py:205
  1.0 6.2 %collective-permute-start = (bf16[8,4224]{1,0:T(8,128)(2,1)S(1)}, bf16[8,4224]{1,0:T(8,128)(2,1)S(1)}, u32[]{:S(2)}, u32[]{:S(2)}) collective-permute-start(bf16[8,4224]{1,0:T(8,128)(2,1)S(1)} %get-tuple-element.17), channel_id=1, source_target_pairs={{0,255},{1,2},{2,1},{3,4},{4,3},{5,6},{6,5},{7,8},{8,7},{9,10},{10... | collective-permute-start | bytes 202760 | tf_op jit(solution)/shard_map/ppermute | solution.py:265
  7.2 0.0 collective-permute-start.1
  7.2 3.1 %shard_map.47 = (f32[7,1280,128]{2,1,0:T(8,128)S(1)}, bf16[33,128,128]{2,1,0:T(8,128)(2,1)S(1)}, bf16[256,256]{1,0:T(8,128)(2,1)S(1)}, bf16[256,256]{1,0:T(8,128)(2,1)S(1)}, f32[8,32,384]{2,1,0:T(8,128)S(1)}) custom-call(s32[7,32]{1,0:T(8,128)S(1)} %get-tuple-element.15.place_v, s32[32]{0:T(128)S(1)} %get-tuple-element.16.agg_v, ...), custom_call_target="tpu_custom_call" | custom-call | tf_op jit(solution)/shard_map/pallas_call | solution.py:220
  10.4 0.0 collective-permute-done.first_ref
  10.4 0.5 %collective-permute-done.1.second_ref = bf16[8,4224]{1,0:T(8,128)(2,1)S(1)} collective-permute-done((bf16[8,4224]{1,0:T(8,128)(2,1)S(1)}, bf16[8,4224]{1,0:T(8,128)(2,1)S(1)}, u32[]{:S(2)}, u32[]{:S(2)}) %collective-permute-start.1) | collective-permute-done | bytes 67616 | tf_op jit(solution)/shard_map/ppermute | solution.py:265
  10.9 2.1 %shard_map.48 = bf16[8,32,320]{2,1,0:T(8,128)(2,1)S(1)} custom-call(s32[7,32]{1,0:T(8,128)S(1)} %get-tuple-element.15.place_v, s32[32]{0:T(128)S(1)} %get-tuple-element.16.agg_v, bf16[8,4224]{1,0:T(8,128)(2,1)S(1)} %collective-permute-done.first_ref, bf16[8,4224]{1,0:T(8,128)(2,1)S(1)} %collective-permute-done.1.second_ref, ...), custom_call_target="tpu_custom_call" | custom-call | tf_op jit(solution)/shard_map/pallas_call | solution.py:243
  13.1 15.8 %all_to_all.5 = bf16[8,32,320]{2,1,0:T(8,128)(2,1)S(1)} all-to-all(bf16[8,32,320]{2,1,0:T(8,128)(2,1)S(1)} %shard_map.48), channel_id=1, replica_groups=mesh['rows'=32,'cols'=8] {'cols'}, dimensions={0} | all-to-all | bytes 327680 | tf_op jit(solution)/shard_map/all_to_all | solution.py:274
  28.9 0.8 %convert.1 = f32[32,8,320]{2,1,0:T(8,128)} convert(bf16[32,8,320]{2,1,0:T(8,128)(2,1)S(1)} %bitcast.3) | non-fusion elementwise | flops 81920 | bytes 491520 | tf_op jit(solution)/shard_map/reshape | solution.py:275
Async XLA Ops:
  1.0 9.4 %collective-permute-start = (bf16[8,4224]{1,0:T(8,128)(2,1)S(1)}, bf16[8,4224]{1,0:T(8,128)(2,1)S(1)}, u32[]{:S(2)}, u32[]{:S(2)}) collective-permute-start(bf16[8,4224]{1,0:T(8,128)(2,1)S(1)} %get-tuple-element.17), channel_id=1, source_target_pairs={{0,255},{1,2},{2,1},{3,4},{4,3},{5,6},{6,5},{7,8},{8,7},{9,10},{10... | collective-permute-start | bytes 202760 | tf_op jit(solution)/shard_map/ppermute | solution.py:265
  7.2 3.7 %collective-permute-start.1 = (bf16[8,4224]{1,0:T(8,128)(2,1)S(1)}, bf16[8,4224]{1,0:T(8,128)(2,1)S(1)}, u32[]{:S(2)}, u32[]{:S(2)}) collective-permute-start(bf16[8,4224]{1,0:T(8,128)(2,1)S(1)} %get-tuple-element.18), channel_id=1, source_target_pairs={{0,1},{1,0},{2,3},{3,2},{4,5},{5,4},{6,7},{7,6},{8,9},{9,8},{10,11... | collective-permute-start | bytes 202760 | tf_op jit(solution)/shard_map/ppermute | solution.py:265

commit v8 on v7

--- a/solution.py
+++ b/solution.py
@@ -192,12 +192,33 @@
         glob[HIGH + t] = jnp.where(t < above, LA, LA + 1)
     products(OUTER, a_nat, w_all, place_s, lambda place, i: glob[place] - agg_s[i] + RC, accs)
     sums = onto_coarse((0, 3), accs, (sel_a, sel_d))
-    for c in range(0, LA, 2):
-        for pair in range(3):
-            lanes = min(128, SL * NS - pair * 128)
-            both = jnp.concatenate([sums[c, pair].reshape(8, 8, 128), sums[c + 1, pair].reshape(8, 8, 128)], axis=1)
-            both = both + part_ref[:, pl.ds(c * 8, 16), pl.ds(pair * 128, 128)]
-            out_ref[:, pl.ds(c * 8, 16), pl.ds(pair * 128, lanes)] = both[:, :, :lanes].astype(jnp.bfloat16)
+    whole = {
+        (c, pair): value.reshape(8, 8, 128) + part_ref[:, pl.ds(c * 8, 8), pl.ds(pair * 128, 128)]
+        for (c, pair), value in sums.items()
+    }
+    for c in range(LA):
+        both = jnp.concatenate([whole[c, 0], whole[c, 1]], axis=1)
+        out_ref[:, pl.ds(c * 16, 16), :] = both.astype(jnp.bfloat16)
+    low = low_lanes(8)[None]
+    tails = [jnp.where(low, whole[c, 2], whole[c + 1, 2]) for c in range(0, LA, 2)]
+    out_ref[:, pl.ds(LA * 16, 16), :] = jnp.concatenate(tails, axis=1).astype(jnp.bfloat16)
+
+
+def unpack_kernel(packed_ref, out_hbm, rows_ref, sems):
+    copies = []
+    for z in range(COLS):
+        packed = packed_ref[z].astype(jnp.float32)
+        for c in range(LA):
+            at = z * LA + c
+            rows_ref[at, :, :128] = packed[c * 16:c * 16 + 8]
+            rows_ref[at, :, 128:256] = packed[c * 16 + 8:c * 16 + 16]
+            tail = packed[LA * 16 + c // 2 * 8:LA * 16 + c // 2 * 8 + 8]
+            rows_ref[at, :, 256:] = (tail if c % 2 == 0 else pltpu.roll(tail, NS, 1))[:, :NS]
+        part = pl.ds(z * LA, LA)
+        copies.append(pltpu.make_async_copy(rows_ref.at[part], out_hbm.at[part], sems.at[z]))
+        copies[z].start()
+    for c in copies:
+        c.wait()
 
 
 def load(prolong, aggregate, columns_t):
@@ -242,7 +263,7 @@
 def outer(place, agg, first, second, *mid):
     return pl.pallas_call(
         outer_kernel,
-        out_shape=shape((COLS, LA * NS // COLS, SL * NS), jnp.bfloat16),
+        out_shape=shape((COLS, LA * 16 + 16, 128), jnp.bfloat16),
         in_specs=[VMEM] * 9,
         out_specs=VMEM,
         scratch_shapes=[
@@ -258,6 +279,18 @@
     )(place, agg, first, second, *mid)
 
 
+def unpack(packed):
+    dims = (COLS * LA, NS // COLS, SL * NS)
+    return pl.pallas_call(
+        unpack_kernel,
+        out_shape=shape(dims, jnp.float32),
+        in_specs=[VMEM],
+        out_specs=HBM,
+        scratch_shapes=[pltpu.VMEM(dims, jnp.float32), pltpu.SemaphoreType.DMA((COLS,))],
+        compiler_params=SMALL,
+    )(packed)
+
+
 def exchanged(shard, first):
     axis = ("rows", "cols")
     length = lax.axis_size(axis)
@@ -272,7 +305,7 @@
     mid = inner(place, agg, p_v, a_blocks)
     mine = outer(place, agg, first, second, *mid)
     landed = lax.all_to_all(mine, "cols", split_axis=0, concat_axis=0, tiled=True)
-    return landed.astype(jnp.float32).reshape(COLS * LA, NS // COLS, SL * NS)
+    return unpack(landed)
 
 
 def solution(mesh):

time: 29.8 us -> 29.2 us (0.980)
  Pallas kernels: 6.26 us -> 7.14 us
  other arithmetic: 0.77 us -> 0 us
  blocking collectives: 15.8 us -> 15.1 us
    pallas_call x1 -> x2, Pallas kernels: 2.13 us -> 3.01 us  [the longest x1 2.14 us: outer(): pl.pallas_call(outer_kernel, out_shape=shape((COLS, LA * 16 + 16, 128), j...]
    reshape x1 -> x0, other arithmetic: 0.77 us -> none  [shards(): return landed.astype(jnp.float32).reshape(COLS * LA, NS // COLS, SL * NS)]
    all_to_all x1, blocking collectives: 15.8 us -> 15.1 us  [shards(): lax.all_to_all(mine, 'cols', split_axis=0, concat_axis=0, tiled=True)]
where the time goes in v8:
time: 29.2 us; the launch traced here: 29 us
  blocking collectives  15.1 us (52%)
  Pallas kernels  7.14 us (24%)
  starting transfers between devices  6.23 us (21%)
  waiting for transfers between devices  0.55 us (2%)
    all_to_all x1, blocking collectives, shards(): lax.all_to_all(mine, 'cols', split_axis=0, concat_axis=0, tiled=True)  15.1 us
    ppermute x2, starting transfers between devices, exchanged(): return lax.ppermute(shard, axis, pairs)  6.23 us
    pallas_call x1, Pallas kernels, inner(): pl.pallas_call(inner_kernel, out_shape=(shape((KN, G * STEP, 128), jnp.fl...  3.13 us
    pallas_call x1, Pallas kernels, outer(): pl.pallas_call(outer_kernel, out_shape=shape((COLS, LA * 16 + 16, 128), j...  2.14 us
    pallas_call x1, Pallas kernels, load(): pl.pallas_call(load_kernel, out_shape=(halo, halo, shape((KN, NB), jnp.in...  1 us
    pallas_call x1, Pallas kernels, unpack(): pl.pallas_call(unpack_kernel, out_shape=shape(dims, jnp.float32), in_spec...  0.87 us
  transfers between devices with their start and end apart: 2, of which 1 were waited for; matrix products, arithmetic and copies ran while one was open for 0% of the time, Pallas kernels for 11%

profile of v8, /device:TPU:31, one launch (start us, length us, event | category | flops | bytes accessed | tf_op | source)
XLA Modules:
  0.0 29.0 jit_solution(4178935845802185456)
XLA Ops:
  0.0 1.0 %shard_map.46 = (bf16[8,4224]{1,0:T(8,128)(2,1)S(1)}, bf16[8,4224]{1,0:T(8,128)(2,1)S(1)}, s32[7,32]{1,0:T(8,128)S(1)}, s32[32]{0:T(128)S(1)}, bf16[32,4096]{1,0:T(8,128)(2,1)S(1)}) custom-call(bf16[32,4096]{1,0:T(8,128)(2,1)} %p_hbm.1, s32[32]{0:T(128)} %agg_hbm.1, s32[7,32]{1,0:T(8,128)} %bitcast.1), custom_call_target="tpu_custom_call" | custom-call | tf_op jit(solution)/shard_map/pallas_call | solution.py:226
  1.0 6.2 %collective-permute-start = (bf16[8,4224]{1,0:T(8,128)(2,1)S(1)}, bf16[8,4224]{1,0:T(8,128)(2,1)S(1)}, u32[]{:S(2)}, u32[]{:S(2)}) collective-permute-start(bf16[8,4224]{1,0:T(8,128)(2,1)S(1)} %get-tuple-element.17), channel_id=1, source_target_pairs={{0,255},{1,2},{2,1},{3,4},{4,3},{5,6},{6,5},{7,8},{8,7},{9,10},{10... | collective-permute-start | bytes 202760 | tf_op jit(solution)/shard_map/ppermute | solution.py:298
  7.2 0.0 collective-permute-start.1
  7.2 3.1 %shard_map.47 = (f32[7,1280,128]{2,1,0:T(8,128)S(1)}, bf16[33,128,128]{2,1,0:T(8,128)(2,1)S(1)}, bf16[256,256]{1,0:T(8,128)(2,1)S(1)}, bf16[256,256]{1,0:T(8,128)(2,1)S(1)}, f32[8,32,384]{2,1,0:T(8,128)S(1)}) custom-call(s32[7,32]{1,0:T(8,128)S(1)} %get-tuple-element.15.place_v, s32[32]{0:T(128)S(1)} %get-tuple-element.16.agg_v, ...), custom_call_target="tpu_custom_call" | custom-call | tf_op jit(solution)/shard_map/pallas_call | solution.py:241
  10.4 0.0 collective-permute-done.first_ref
  10.4 0.5 %collective-permute-done.1.second_ref = bf16[8,4224]{1,0:T(8,128)(2,1)S(1)} collective-permute-done((bf16[8,4224]{1,0:T(8,128)(2,1)S(1)}, bf16[8,4224]{1,0:T(8,128)(2,1)S(1)}, u32[]{:S(2)}, u32[]{:S(2)}) %collective-permute-start.1) | collective-permute-done | bytes 67616 | tf_op jit(solution)/shard_map/ppermute | solution.py:298
  10.9 2.1 %shard_map.48 = bf16[8,80,128]{2,1,0:T(8,128)(2,1)S(1)} custom-call(s32[7,32]{1,0:T(8,128)S(1)} %get-tuple-element.15.place_v, s32[32]{0:T(128)S(1)} %get-tuple-element.16.agg_v, bf16[8,4224]{1,0:T(8,128)(2,1)S(1)} %collective-permute-done.first_ref, bf16[8,4224]{1,0:T(8,128)(2,1)S(1)} %collective-permute-done.1.second_ref, ...), custom_call_target="tpu_custom_call" | custom-call | tf_op jit(solution)/shard_map/pallas_call | solution.py:264
  13.1 15.1 %all_to_all.5.packed_ref = bf16[8,80,128]{2,1,0:T(8,128)(2,1)S(1)} all-to-all(bf16[8,80,128]{2,1,0:T(8,128)(2,1)S(1)} %shard_map.48), channel_id=1, replica_groups=mesh['rows'=32,'cols'=8] {'cols'}, dimensions={0} | all-to-all | bytes 327680 | tf_op jit(solution)/shard_map/all_to_all | solution.py:307
  28.2 0.9 %shard_map.49 = f32[32,8,320]{2,1,0:T(8,128)} custom-call(bf16[8,80,128]{2,1,0:T(8,128)(2,1)S(1)} %all_to_all.5.packed_ref), custom_call_target="tpu_custom_call" | custom-call | tf_op jit(solution)/shard_map/pallas_call | solution.py:284
Async XLA Ops:
  1.0 9.4 %collective-permute-start = (bf16[8,4224]{1,0:T(8,128)(2,1)S(1)}, bf16[8,4224]{1,0:T(8,128)(2,1)S(1)}, u32[]{:S(2)}, u32[]{:S(2)}) collective-permute-start(bf16[8,4224]{1,0:T(8,128)(2,1)S(1)} %get-tuple-element.17), channel_id=1, source_target_pairs={{0,255},{1,2},{2,1},{3,4},{4,3},{5,6},{6,5},{7,8},{8,7},{9,10},{10... | collective-permute-start | bytes 202760 | tf_op jit(solution)/shard_map/ppermute | solution.py:298
  7.2 3.7 %collective-permute-start.1 = (bf16[8,4224]{1,0:T(8,128)(2,1)S(1)}, bf16[8,4224]{1,0:T(8,128)(2,1)S(1)}, u32[]{:S(2)}, u32[]{:S(2)}) collective-permute-start(bf16[8,4224]{1,0:T(8,128)(2,1)S(1)} %get-tuple-element.18), channel_id=1, source_target_pairs={{0,1},{1,0},{2,3},{3,2},{4,5},{5,4},{6,7},{7,6},{8,9},{9,8},{10,11... | collective-permute-start | bytes 202760 | tf_op jit(solution)/shard_map/ppermute | solution.py:298

commit v9 on v8

--- a/solution.py
+++ b/solution.py
@@ -99,9 +99,12 @@
     for at, group in enumerate(groups):
         first, count = IDS[group]
         mine = accs[at * 8:at * 8 + 8]
-        rows = [jnp.concatenate([acc[s] for s in range(SL)], axis=1).astype(jnp.bfloat16) for acc in mine]
-        full = lax.dot_general(jnp.concatenate(rows, axis=0), sels[at][...], (((0,), (0,)), ((), ())),
-                               preferred_element_type=jnp.float32)
+        parts = [
+            lax.dot_general(jnp.concatenate([acc[s].astype(jnp.bfloat16) for acc in mine], axis=0), sels[at][...],
+                            (((0,), (0,)), ((), ())), preferred_element_type=jnp.float32)
+            for s in range(SL)
+        ]
+        full = jnp.concatenate(parts, axis=0)
         for c in range(count):
             cc = full[:, c * 128:(c + 1) * 128]
             part = lambda s, par: cc[s * 128 + par * NS:s * 128 + (par + 1) * NS]

time: 29.2 us -> 29.1 us (level)
  no operation moved by 1% of the time
where the time goes in v9:
time: 29.1 us; the launch traced here: 29 us
  blocking collectives  15.1 us (52%)
  Pallas kernels  7.09 us (24%)
  starting transfers between devices  6.23 us (21%)
  waiting for transfers between devices  0.54 us (2%)
    all_to_all x1, blocking collectives, shards(): lax.all_to_all(mine, 'cols', split_axis=0, concat_axis=0, tiled=True)  15.1 us
    ppermute x2, starting transfers between devices, exchanged(): return lax.ppermute(shard, axis, pairs)  6.23 us
    pallas_call x1, Pallas kernels, inner(): pl.pallas_call(inner_kernel, out_shape=(shape((KN, G * STEP, 128), jnp.fl...  3.14 us
    pallas_call x1, Pallas kernels, outer(): pl.pallas_call(outer_kernel, out_shape=shape((COLS, LA * 16 + 16, 128), j...  2.08 us
    pallas_call x1, Pallas kernels, load(): pl.pallas_call(load_kernel, out_shape=(halo, halo, shape((KN, NB), jnp.in...  1 us
    pallas_call x1, Pallas kernels, unpack(): pl.pallas_call(unpack_kernel, out_shape=shape(dims, jnp.float32), in_spec...  0.87 us
  transfers between devices with their start and end apart: 2, of which 1 were waited for; matrix products, arithmetic and copies ran while one was open for 0% of the time, Pallas kernels for 11%

profile of v9, /device:TPU:31, one launch (start us, length us, event | category | flops | bytes accessed | tf_op | source)
XLA Modules:
  0.0 29.0 jit_solution(7165899473363420534)
XLA Ops:
  0.0 1.0 %shard_map.46 = (bf16[8,4224]{1,0:T(8,128)(2,1)S(1)}, bf16[8,4224]{1,0:T(8,128)(2,1)S(1)}, s32[7,32]{1,0:T(8,128)S(1)}, s32[32]{0:T(128)S(1)}, bf16[32,4096]{1,0:T(8,128)(2,1)S(1)}) custom-call(bf16[32,4096]{1,0:T(8,128)(2,1)} %p_hbm.1, s32[32]{0:T(128)} %agg_hbm.1, s32[7,32]{1,0:T(8,128)} %bitcast.1), custom_call_target="tpu_custom_call" | custom-call | tf_op jit(solution)/shard_map/pallas_call | solution.py:229
  1.0 6.2 %collective-permute-start = (bf16[8,4224]{1,0:T(8,128)(2,1)S(1)}, bf16[8,4224]{1,0:T(8,128)(2,1)S(1)}, u32[]{:S(2)}, u32[]{:S(2)}) collective-permute-start(bf16[8,4224]{1,0:T(8,128)(2,1)S(1)} %get-tuple-element.17), channel_id=1, source_target_pairs={{0,255},{1,2},{2,1},{3,4},{4,3},{5,6},{6,5},{7,8},{8,7},{9,10},{10... | collective-permute-start | bytes 202760 | tf_op jit(solution)/shard_map/ppermute | solution.py:301
  7.2 0.0 collective-permute-start.1
  7.2 3.1 %shard_map.47 = (f32[7,1280,128]{2,1,0:T(8,128)S(1)}, bf16[33,128,128]{2,1,0:T(8,128)(2,1)S(1)}, bf16[256,256]{1,0:T(8,128)(2,1)S(1)}, bf16[256,256]{1,0:T(8,128)(2,1)S(1)}, f32[8,32,384]{2,1,0:T(8,128)S(1)}) custom-call(s32[7,32]{1,0:T(8,128)S(1)} %get-tuple-element.15.place_v, s32[32]{0:T(128)S(1)} %get-tuple-element.16.agg_v, ...), custom_call_target="tpu_custom_call" | custom-call | tf_op jit(solution)/shard_map/pallas_call | solution.py:244
  10.4 0.0 collective-permute-done.first_ref
  10.4 0.5 %collective-permute-done.1.second_ref = bf16[8,4224]{1,0:T(8,128)(2,1)S(1)} collective-permute-done((bf16[8,4224]{1,0:T(8,128)(2,1)S(1)}, bf16[8,4224]{1,0:T(8,128)(2,1)S(1)}, u32[]{:S(2)}, u32[]{:S(2)}) %collective-permute-start.1) | collective-permute-done | bytes 67616 | tf_op jit(solution)/shard_map/ppermute | solution.py:301
  10.9 2.1 %shard_map.48 = bf16[8,80,128]{2,1,0:T(8,128)(2,1)S(1)} custom-call(s32[7,32]{1,0:T(8,128)S(1)} %get-tuple-element.15.place_v, s32[32]{0:T(128)S(1)} %get-tuple-element.16.agg_v, bf16[8,4224]{1,0:T(8,128)(2,1)S(1)} %collective-permute-done.first_ref, bf16[8,4224]{1,0:T(8,128)(2,1)S(1)} %collective-permute-done.1.second_ref, ...), custom_call_target="tpu_custom_call" | custom-call | tf_op jit(solution)/shard_map/pallas_call | solution.py:267
  13.0 15.1 %all_to_all.5.packed_ref = bf16[8,80,128]{2,1,0:T(8,128)(2,1)S(1)} all-to-all(bf16[8,80,128]{2,1,0:T(8,128)(2,1)S(1)} %shard_map.48), channel_id=1, replica_groups=mesh['rows'=32,'cols'=8] {'cols'}, dimensions={0} | all-to-all | bytes 327680 | tf_op jit(solution)/shard_map/all_to_all | solution.py:310
  28.1 0.9 %shard_map.49 = f32[32,8,320]{2,1,0:T(8,128)} custom-call(bf16[8,80,128]{2,1,0:T(8,128)(2,1)S(1)} %all_to_all.5.packed_ref), custom_call_target="tpu_custom_call" | custom-call | tf_op jit(solution)/shard_map/pallas_call | solution.py:287
Async XLA Ops:
  1.0 9.4 %collective-permute-start = (bf16[8,4224]{1,0:T(8,128)(2,1)S(1)}, bf16[8,4224]{1,0:T(8,128)(2,1)S(1)}, u32[]{:S(2)}, u32[]{:S(2)}) collective-permute-start(bf16[8,4224]{1,0:T(8,128)(2,1)S(1)} %get-tuple-element.17), channel_id=1, source_target_pairs={{0,255},{1,2},{2,1},{3,4},{4,3},{5,6},{6,5},{7,8},{8,7},{9,10},{10... | collective-permute-start | bytes 202760 | tf_op jit(solution)/shard_map/ppermute | solution.py:301
  7.2 3.7 %collective-permute-start.1 = (bf16[8,4224]{1,0:T(8,128)(2,1)S(1)}, bf16[8,4224]{1,0:T(8,128)(2,1)S(1)}, u32[]{:S(2)}, u32[]{:S(2)}) collective-permute-start(bf16[8,4224]{1,0:T(8,128)(2,1)S(1)} %get-tuple-element.18), channel_id=1, source_target_pairs={{0,1},{1,0},{2,3},{3,2},{4,5},{5,4},{6,7},{7,6},{8,9},{9,8},{10,11... | collective-permute-start | bytes 202760 | tf_op jit(solution)/shard_map/ppermute | solution.py:301

commit v10 on v8

--- a/solution.py
+++ b/solution.py
@@ -84,8 +84,8 @@
     wide[pl.ds(BW + 1, G, stride=2), :] = odd
 
 
-def products(rows, a_nat, w_ref, place_s, slot_of, accs):
-    for k in range(KN):
+def products(rows, a_nat, w_ref, place_s, slot_of, accs, entries=range(KN)):
+    for k in entries:
         for i, acc in zip(rows, accs):
             block = a_nat[k, pl.ds(i, G, stride=STEP), :].astype(jnp.bfloat16)
             place = place_s[k, i]
@@ -147,12 +147,13 @@
         lane = pl.multiple_of((agg_s[j] - IDS[j // 8][0]) * 128, 128)
         sels[j // 8][pl.ds(j % 8 * G, G), pl.ds(lane, 128)] = nat.astype(jnp.bfloat16)
     w_ref[NONE] = jnp.zeros((128, 128), jnp.bfloat16)
-    for k in range(KN):
-        a_in[k].wait()
-        for g in range(G):
-            a_nat[k, pl.ds(g * STEP, NB), :] = a_ref[:, pl.ds(k * BLK + g * 128, 128)].astype(jnp.float32)
-
-    products(INNER, a_nat, w_ref, place_s, lambda place, i: glob[place] - agg_s[i] + RC, accs)
+
+    for entries in (range(3), range(3, KN)):
+        for k in entries:
+            a_in[k].wait()
+            for g in range(G):
+                a_nat[k, pl.ds(g * STEP, NB), :] = a_ref[:, pl.ds(k * BLK + g * 128, 128)].astype(jnp.float32)
+        products(INNER, a_nat, w_ref, place_s, lambda place, i: glob[place] - agg_s[i] + RC, accs, entries)
     for (c, pair), value in onto_coarse((1, 2), accs, (sel_b, sel_c)).items():
         part_ref[:, pl.ds(c * 8, 8), pl.ds(pair * 128, 128)] = value.reshape(8, 8, 128)
 

time: 29.2 us -> 29.2 us (level)
  no operation moved by 1% of the time
where the time goes in v10:
time: 29.2 us; the launch traced here: 29 us
  blocking collectives  15.1 us (52%)
  Pallas kernels  7.11 us (24%)
  starting transfers between devices  6.23 us (21%)
  waiting for transfers between devices  0.57 us (2%)
    all_to_all x1, blocking collectives, shards(): lax.all_to_all(mine, 'cols', split_axis=0, concat_axis=0, tiled=True)  15.1 us
    ppermute x2, starting transfers between devices, exchanged(): return lax.ppermute(shard, axis, pairs)  6.23 us
    pallas_call x1, Pallas kernels, inner(): pl.pallas_call(inner_kernel, out_shape=(shape((KN, G * STEP, 128), jnp.fl...  3.11 us
    pallas_call x1, Pallas kernels, outer(): pl.pallas_call(outer_kernel, out_shape=shape((COLS, LA * 16 + 16, 128), j...  2.14 us
    pallas_call x1, Pallas kernels, load(): pl.pallas_call(load_kernel, out_shape=(halo, halo, shape((KN, NB), jnp.in...  1 us
    pallas_call x1, Pallas kernels, unpack(): pl.pallas_call(unpack_kernel, out_shape=shape(dims, jnp.float32), in_spec...  0.87 us
  transfers between devices with their start and end apart: 2, of which 1 were waited for; matrix products, arithmetic and copies ran while one was open for 0% of the time, Pallas kernels for 11%

profile of v10, /device:TPU:31, one launch (start us, length us, event | category | flops | bytes accessed | tf_op | source)
XLA Modules:
  0.0 29.0 jit_solution(10654625947751046257)
XLA Ops:
  0.0 1.0 %shard_map.46 = (bf16[8,4224]{1,0:T(8,128)(2,1)S(1)}, bf16[8,4224]{1,0:T(8,128)(2,1)S(1)}, s32[7,32]{1,0:T(8,128)S(1)}, s32[32]{0:T(128)S(1)}, bf16[32,4096]{1,0:T(8,128)(2,1)S(1)}) custom-call(bf16[32,4096]{1,0:T(8,128)(2,1)} %p_hbm.1, s32[32]{0:T(128)} %agg_hbm.1, s32[7,32]{1,0:T(8,128)} %bitcast.1), custom_call_target="tpu_custom_call" | custom-call | tf_op jit(solution)/shard_map/pallas_call | solution.py:227
  1.0 6.2 %collective-permute-start = (bf16[8,4224]{1,0:T(8,128)(2,1)S(1)}, bf16[8,4224]{1,0:T(8,128)(2,1)S(1)}, u32[]{:S(2)}, u32[]{:S(2)}) collective-permute-start(bf16[8,4224]{1,0:T(8,128)(2,1)S(1)} %get-tuple-element.17), channel_id=1, source_target_pairs={{0,255},{1,2},{2,1},{3,4},{4,3},{5,6},{6,5},{7,8},{8,7},{9,10},{10... | collective-permute-start | bytes 202760 | tf_op jit(solution)/shard_map/ppermute | solution.py:299
  7.2 0.0 collective-permute-start.1
  7.2 3.1 %shard_map.47 = (f32[7,1280,128]{2,1,0:T(8,128)S(1)}, bf16[33,128,128]{2,1,0:T(8,128)(2,1)S(1)}, bf16[256,256]{1,0:T(8,128)(2,1)S(1)}, bf16[256,256]{1,0:T(8,128)(2,1)S(1)}, f32[8,32,384]{2,1,0:T(8,128)S(1)}) custom-call(s32[7,32]{1,0:T(8,128)S(1)} %get-tuple-element.15.place_v, s32[32]{0:T(128)S(1)} %get-tuple-element.16.agg_v, ...), custom_call_target="tpu_custom_call" | custom-call | tf_op jit(solution)/shard_map/pallas_call | solution.py:242
  10.3 0.0 collective-permute-done.first_ref
  10.4 0.6 %collective-permute-done.1.second_ref = bf16[8,4224]{1,0:T(8,128)(2,1)S(1)} collective-permute-done((bf16[8,4224]{1,0:T(8,128)(2,1)S(1)}, bf16[8,4224]{1,0:T(8,128)(2,1)S(1)}, u32[]{:S(2)}, u32[]{:S(2)}) %collective-permute-start.1) | collective-permute-done | bytes 67616 | tf_op jit(solution)/shard_map/ppermute | solution.py:299
  10.9 2.1 %shard_map.48 = bf16[8,80,128]{2,1,0:T(8,128)(2,1)S(1)} custom-call(s32[7,32]{1,0:T(8,128)S(1)} %get-tuple-element.15.place_v, s32[32]{0:T(128)S(1)} %get-tuple-element.16.agg_v, bf16[8,4224]{1,0:T(8,128)(2,1)S(1)} %collective-permute-done.first_ref, bf16[8,4224]{1,0:T(8,128)(2,1)S(1)} %collective-permute-done.1.second_ref, ...), custom_call_target="tpu_custom_call" | custom-call | tf_op jit(solution)/shard_map/pallas_call | solution.py:265
  13.1 15.1 %all_to_all.5.packed_ref = bf16[8,80,128]{2,1,0:T(8,128)(2,1)S(1)} all-to-all(bf16[8,80,128]{2,1,0:T(8,128)(2,1)S(1)} %shard_map.48), channel_id=1, replica_groups=mesh['rows'=32,'cols'=8] {'cols'}, dimensions={0} | all-to-all | bytes 327680 | tf_op jit(solution)/shard_map/all_to_all | solution.py:308
  28.2 0.9 %shard_map.49 = f32[32,8,320]{2,1,0:T(8,128)} custom-call(bf16[8,80,128]{2,1,0:T(8,128)(2,1)S(1)} %all_to_all.5.packed_ref), custom_call_target="tpu_custom_call" | custom-call | tf_op jit(solution)/shard_map/pallas_call | solution.py:285
Async XLA Ops:
  1.0 9.3 %collective-permute-start = (bf16[8,4224]{1,0:T(8,128)(2,1)S(1)}, bf16[8,4224]{1,0:T(8,128)(2,1)S(1)}, u32[]{:S(2)}, u32[]{:S(2)}) collective-permute-start(bf16[8,4224]{1,0:T(8,128)(2,1)S(1)} %get-tuple-element.17), channel_id=1, source_target_pairs={{0,255},{1,2},{2,1},{3,4},{4,3},{5,6},{6,5},{7,8},{8,7},{9,10},{10... | collective-permute-start | bytes 202760 | tf_op jit(solution)/shard_map/ppermute | solution.py:299
  7.2 3.7 %collective-permute-start.1 = (bf16[8,4224]{1,0:T(8,128)(2,1)S(1)}, bf16[8,4224]{1,0:T(8,128)(2,1)S(1)}, u32[]{:S(2)}, u32[]{:S(2)}) collective-permute-start(bf16[8,4224]{1,0:T(8,128)(2,1)S(1)} %get-tuple-element.18), channel_id=1, source_target_pairs={{0,1},{1,0},{2,3},{3,2},{4,5},{5,4},{6,7},{7,6},{8,9},{9,8},{10,11... | collective-permute-start | bytes 202760 | tf_op jit(solution)/shard_map/ppermute | solution.py:299
